TPU v7x, 32 devices: a whole 2x2x4 slice. The times are simulated.
32 devices in a mesh: gx: 8 (over y, x, core), gy: 4 (over z).
Axes of the slice: x: 2, y: 2, z: 4, core: 2. Of those that a mesh axis runs over, the one named last changes fastest.
Arguments:
- diag_blocks: float32 [9, 512, 512], P(None, 'gx', 'gy'), may hold values from 0 to 36, as said below
- edge_blocks: float32 [4, 9, 512, 512], P(None, None, 'gx', 'gy'), may hold values from -0.3 to 0.3
- edge_mask: int32 [4, 512, 512], P(None, 'gx', 'gy'), may hold values 0 or 1
- src_values: float32 [3, 32768], P(None, ('gx', 'gy')), may hold values from -48 to 48
- src_owner: int32 [32768, 1], P(('gx', 'gy')), may hold values from 0 to 7; in each aligned block of 1024 rows (0 to 1023, 1024 to 2047, ...) at most 256 rows name the same one
- src_node: int32 [32768], P(('gx', 'gy')), may hold values from 0 to 8191
- src_count: int32 [32], P(('gx', 'gy')), may hold values from 256 to 1024, as said below
- surf_node: int32 [65536], P(('gx', 'gy')), may hold values from 0 to 8191
- surf_param: float32 [3, 65536], P(None, ('gx', 'gy')), may hold values from 0 to 1
- tile_box: int32 [512], P(('gx', 'gy')), may hold values from 0 to 31
Outputs:
- adjoint_field: float32 [3, 512, 512], P(None, 'gx', 'gy')
- box_gradient: float32 [32, 192], P(('gx', 'gy'))
Inputs may be any that keep to these rules, and one draw needn't show every extreme that they name: `src_owner`: each device's rows name every gx index at most 256 times. `src_count`: some device has all 1024 rows live. `diag_blocks`: entries 0, 4 and 8 lie between 6 and 36; the other entries between 0 and 1.
All inputs are finite; a program needn't handle non-finite values. No bound on the sum of `edge_mask` on one device may be relied on, other than what follows from the above.
Results may differ from a plain program's by a relative error of at most 0.0015.
Values sent between devices are 32-bit elements; how exact they have to be, the bound alone decides.
No kernel may reach another device: no remote copies, remote signals or barrier semaphores. Data moves between devices by JAX's collectives and lax.ppermute only.
A program may use at most 64 MiB of HBM per device.

v0:
```python
import functools
import math

import jax
import jax.numpy as jnp
from jax import lax
from jax.experimental import pallas as pl
from jax.experimental.pallas import tpu as pltpu
from jax.sharding import PartitionSpec as P

F32 = jnp.float32
BF16 = jnp.bfloat16
PAD = 2
NOWHERE = -(1 << 20)
LANES = 128
NEAR = 16
STRIP = 40
CHUNK = 256
PARAMS = pltpu.CompilerParams(vmem_limit_bytes=24 * 1024 * 1024)

VMEM = pl.BlockSpec(memory_space=pltpu.VMEM)
SMEM = pl.BlockSpec(memory_space=pltpu.SMEM)
HBM = pl.BlockSpec(memory_space=pltpu.HBM)


def iota(shape, dim):
    return lax.broadcasted_iota(jnp.int32, shape, dim)


def float_iota(shape, dim):
    return iota(shape, dim).astype(F32)


def two_parts(value):
    high = value.astype(BF16).astype(F32)
    return high, value - high


def product(block, field):
    return [
        block(row) * field[0] + block(3 + row) * field[1] + block(6 + row) * field[2]
        for row in range(3)
    ]


def off_diagonal(block, field):
    return [
        sum(block(3 * i + row) * field[i] for i in range(3) if i != row) for row in range(3)
    ]


def masked_product(edge_ref, mask_ref, direction, field):
    mask = mask_ref[direction].astype(F32)
    return [mask * part for part in product(lambda k: edge_ref[direction, k], field)]


def rows_moved(field, edge_row, step):
    size = field.shape[0]
    at = iota(field.shape, 0)
    moved = pltpu.roll(field, step % size, 0)
    return jnp.where(at == (0 if step == 1 else size - 1), edge_row, moved)


def lanes_moved(field, edge_column, step):
    size = field.shape[1]
    at = iota(field.shape, 1)
    moved = pltpu.roll(field, step % size, 1)
    return jnp.where(at == (0 if step == 1 else size - 1), edge_column, moved)


def pack_kernel(
    count_ref, values_in, owner_in, node_in, diag_in, edge_in, mask_in, rows_out, strip_ref,
    values_ref, owner_ref, node_ref, diag_low, diag_high, edge_low, edge_high,
    mask_low, mask_high, rows_ref, arrived, left,
):
    targets = rows_ref.shape[0]
    groups = owner_ref.shape[0]
    cells_x = diag_in.shape[1]
    top = pl.ds(cells_x - 8, 8)
    copies = [
        pltpu.make_async_copy(source, target, arrived.at[k])
        for k, (source, target) in enumerate(
            (
                (owner_in, owner_ref),
                (node_in, node_ref),
                (values_in, values_ref),
                (diag_in.at[:, 0:8], diag_low),
                (diag_in.at[:, top], diag_high),
                (mask_in.at[1, 0:8], mask_low),
                (mask_in.at[:, top], mask_high),
                (edge_in.at[1, :, 0:8], edge_low),
                (edge_in.at[:, :, top], edge_high),
            )
        )
    ]
    for copy in copies:
        copy.start()
    base = 4 * groups
    for target in range(targets):
        rows_ref[target, base:, :] = jnp.zeros((NEAR, LANES), F32)
    for copy in copies[:2]:
        copy.wait()
    order = iota((groups, LANES), 0) * LANES + iota((groups, LANES), 1)
    node = node_ref[...]
    frame = cells_x + 2 * PAD
    row = owner_ref[...] * cells_x + lax.shift_right_logical(node, 7)
    row = jnp.where(order < count_ref[0], row, NOWHERE)
    column = node & (LANES - 1)
    for target in range(targets):
        line = row - (target * cells_x - PAD)
        inside = (line >= 0) & (line < frame)
        index = jnp.where(inside, line * LANES + column, -1)
        rows_ref[target, 3 * groups : 4 * groups, :] = index.astype(F32)

    copies[2].wait()
    for comp in range(3):
        value = jnp.concatenate(
            [
                values_ref[comp : comp + 1, group * LANES : (group + 1) * LANES]
                for group in range(groups)
            ],
            axis=0,
        )
        for target in range(targets):
            rows_ref[target, comp * groups : (comp + 1) * groups, :] = value
    near = pl.ds(4 * groups, NEAR)
    leaving = [
        pltpu.make_async_copy(rows_ref.at[:, part], rows_out.at[:, part], left.at[k])
        for k, part in enumerate((pl.ds(0, 4 * groups), near))
    ]
    leaving[0].start()
    for copy in copies[3:]:
        copy.wait()

    def block(edge, mask, direction, at):
        present = mask[direction, at : at + 1, :].astype(F32)
        return [edge[direction, k, at : at + 1, :] * present for k in range(9)]

    up_y, low_y = block(edge_high, mask_high, 2, 7), block(edge_high, mask_high, 3, 7)
    here = lax.axis_index("gx")

    @pl.when(here < targets - 1)
    def _():
        def put(slot, value):
            rows_ref[here + 1, base + slot : base + slot + 1, :] = value

        for k in range(3):
            put(k, diag_high[4 * k, 7:8, :])
        for k, value in enumerate(block(edge_high, mask_high, 0, 7)):
            put(3 + k, value)
        corners = jnp.zeros((1, LANES), F32)
        lane = iota((1, LANES), 1)
        for k in range(9):
            corners = jnp.where(lane == k, up_y[k][:, LANES - 1 :], corners)
            corners = jnp.where(lane == 9 + k, low_y[k][:, :1], corners)
        put(12, corners)

    @pl.when(here > 0)
    def _():
        def put(slot, value):
            rows_ref[here - 1, base + slot : base + slot + 1, :] = value

        for k in range(3):
            put(k, diag_low[4 * k, 0:1, :])
        present = mask_low[0:1, :].astype(F32)
        for k in range(9):
            put(3 + k, edge_low[k, 0:1, :] * present)

    leaving[1].start()
    later = [diag_high[k, 7:8, :] for k in range(9) if k % 4]
    later += up_y + low_y + block(edge_high, mask_high, 0, 6)
    later += [diag_high[4 * k, 6:7, :] for k in range(3)]
    for k, value in enumerate(later):
        strip_ref[k : k + 1, :] = value
    strip_ref[len(later) :, :] = jnp.zeros((STRIP - len(later), LANES), F32)
    for copy in leaving:
        copy.wait()


def stretched(row, count):
    tile = jnp.broadcast_to(row, (16, row.shape[1])).astype(BF16)
    return jnp.concatenate([tile] * (count // 16), axis=0)


def ratio(value, scale):
    return jnp.where(scale > 0.0, value / jnp.where(scale > 0.0, scale, 1.0), 0.0)


UP_X, LOW_X, INWARD, OUTWARD, WITHIN, INVERSE = 0, 3, 6, 9, 12, 15


def edge_kernel(diag_ref, edge_ref, mask_ref, inverse_ref, columns_ref):
    cells_x = diag_ref.shape[1]
    at = iota((cells_x, LANES), 1)
    sides = [jnp.zeros((cells_x, LANES), F32) for _ in range(2)]

    def put(kind, i, a, first, first_lane, last, last_lane):
        slot = 8 * (kind + i) + a
        for side, (field, lane) in enumerate(((first, first_lane), (last, last_lane))):
            sides[side] = jnp.where(at == slot, field[:, lane : lane + 1], sides[side])

    inverse = [1.0 / diag_ref[4 * c] for c in range(3)]
    end = LANES - 1
    masks = [mask_ref[direction].astype(F32) for direction in range(4)]
    for i in range(3):
        inverse_ref[i] = inverse[i]
        put(INVERSE, 0, i, inverse[i], 0, inverse[i], end)
        for a in range(3):
            up_x, low_x, up_y, low_y = (
                edge_ref[direction, 3 * i + a] * masks[direction] for direction in range(4)
            )
            put(UP_X, i, a, up_x, 0, up_x, end)
            put(LOW_X, i, a, low_x, 0, low_x, end)
            put(INWARD, i, a, low_y, 1, up_y, end - 1)
            put(OUTWARD, i, a, low_y, 0, up_y, end)
            if a != i:
                put(WITHIN, i, a, diag_ref[3 * i + a], 0, diag_ref[3 * i + a], end)
    columns_ref[...] = jnp.concatenate(sides, axis=0).T


def field_kernel(
    rows_ref, inverse_ref, columns_ref,
    field_ref, halo_ref, inner_ref, outer_ref, load_ref,
):
    senders = rows_ref.shape[0]
    groups = (rows_ref.shape[1] - NEAR) // 4
    cells_x = field_ref.shape[1]
    half = (cells_x + 2 * PAD) // 2
    own = cells_x // 2

    load_ref[...] = jnp.zeros_like(load_ref)
    here = lax.axis_index("gx")

    size = load_ref.shape[0]
    line = iota((size, LANES), 0)
    block = sum(jnp.where(line >= half * k, 1, 0) for k in range(1, 6))
    at_row = jnp.where(line < 6 * half, line - half * block, -5).astype(F32).astype(BF16)
    at_column = float_iota((2 * LANES, LANES), 0).astype(BF16)
    in_tile = float_iota((16, LANES), 0).astype(BF16)
    zero, one = jnp.zeros((), BF16), jnp.ones((), BF16)

    def operands(sender):
        index = rows_ref[sender, 3 * groups : 4 * groups, :]
        split = float(half * LANES)
        index, shift = (
            jnp.where(index >= split, index - split, index),
            jnp.where(index >= split, float(LANES), 0.0),
        )
        place = jnp.floor(index * (1.0 / LANES))
        column = index - place * float(LANES) + shift
        parts = [
            two_parts(rows_ref[sender, c * groups : (c + 1) * groups, :]) for c in range(3)
        ]
        lefts, rights = [], []
        for group in range(groups):
            line = slice(group, group + 1)
            values = [
                stretched(parts[c][which][line], 16) for which in range(2) for c in range(3)
            ]
            tiles = []
            for first in range(0, size, 16):
                low, high = first // half, min((first + 15) // half, 5)
                tiles.append(
                    values[low]
                    if low == high
                    else jnp.where(
                        in_tile < float(half * high - first), values[low], values[high]
                    )
                )
            match = at_row == stretched(place[line], size)
            lefts.append(jnp.where(match, jnp.concatenate(tiles, axis=0), zero))
            rights.append(
                jnp.where(at_column == stretched(column[line], 2 * LANES), one, zero)
            )
        return lefts, rights

    together = math.gcd(senders, 4)

    def add_rows(step, carry):
        lefts, rights = [], []
        for k in range(together):
            left, right = operands(step * together + k)
            lefts += left
            rights += right
        load_ref[...] += lax.dot_general(
            jnp.concatenate(lefts, axis=1),
            jnp.concatenate(rights, axis=1),
            (((1,), (1,)), ((), ())),
            preferred_element_type=F32,
        )
        return carry

    steps = senders // together
    lax.fori_loop(0, steps, add_rows, 0, unroll=min(steps, 2))

    def load_rows(comp, first, last, second_half):
        lanes = slice(LANES, 2 * LANES) if second_half else slice(0, LANES)
        return (
            load_ref[comp * half + first : comp * half + last, lanes]
            + load_ref[(3 + comp) * half + first : (3 + comp) * half + last, lanes]
        )

    field = []
    for comp in range(3):
        load = jnp.concatenate(
            [load_rows(comp, PAD, half, False), load_rows(comp, 0, half - PAD, True)], axis=0
        )
        field.append(load * inverse_ref[comp])
        field_ref[comp] = field[comp]
    beyond = half - PAD
    near_before = [load_rows(c, PAD - 1, PAD, False) for c in range(3)]
    far_before = [load_rows(c, PAD - 2, PAD - 1, False) for c in range(3)]
    near_after = [load_rows(c, beyond, beyond + 1, True) for c in range(3)]

    base = 4 * groups

    def neighbour(sender, load):
        def entry(k):
            return rows_ref[sender, base + k : base + k + 1, :]

        inverse = [ratio(1.0, entry(k)) for k in range(3)]
        toward = [entry(3 + k) for k in range(9)]
        beside = [load[c] * inverse[c] for c in range(3)]
        return inverse, toward, beside, product(lambda k: toward[k], beside)

    lower = jnp.maximum(here - 1, 0)
    before = neighbour(lower, near_before)
    after = neighbour(jnp.minimum(here + 1, senders - 1), near_after)
    rows = before[2] + before[0] + before[3] + before[1] + far_before + after[3]
    for k, value in enumerate(rows):
        halo_ref[k : k + 1, :] = value
    lane_row = iota((1, LANES), 1)
    ends = jnp.zeros((1, LANES), F32)
    for i in range(3):
        for a in range(3):
            ends = jnp.where(lane_row == 3 * i + a, before[2][i][:, LANES - 1 :], ends)
            ends = jnp.where(lane_row == 9 + 3 * i + a, before[2][i][:, :1], ends)
    ends = ends * rows_ref[lower, base + 12 : base + 13, :]
    ends = ends + pltpu.roll(ends, LANES - 3, 1) + pltpu.roll(ends, LANES - 6, 1)

    at = iota((cells_x, LANES), 1)
    sides = []
    for edge, inside in ((0, 1), (LANES - 1, LANES - 2)):
        packed = jnp.zeros((cells_x, LANES), F32)
        for comp in range(3):
            packed = jnp.where(at == comp, field[comp][:, edge : edge + 1], packed)
            packed = jnp.where(at == 8 + comp, field[comp][:, inside : inside + 1], packed)
        sides.append(packed)
    turned = jnp.concatenate(sides, axis=0).T

    def column_product(kind, first):
        return sum(
            columns_ref[8 * (kind + i) : 8 * (kind + i) + 8, :] * turned[first + i : first + i + 1]
            for i in range(3)
        )

    def eight(rows):
        return jnp.concatenate(rows + [jnp.zeros((8 - len(rows), LANES), F32)], axis=0)

    lane = iota((8, LANES), 1)
    from_before, from_after = eight(before[3]), eight(after[3])
    from_before = jnp.where(lane == 0, from_before, pltpu.roll(from_before, cells_x + 1, 1))
    from_after = jnp.where(
        lane == LANES - 1, from_after, pltpu.roll(from_after, cells_x - 1, 1)
    )
    row = lane & (cells_x - 1)
    upward = pltpu.roll(column_product(UP_X, 0), 1, 1)
    downward = pltpu.roll(column_product(LOW_X, 0), LANES - 1, 1)
    total = (
        column_product(WITHIN, 0)
        + jnp.where(row == 0, from_before, upward)
        + jnp.where(row == cells_x - 1, from_after, downward)
        + column_product(INWARD, 8)
    )
    inverse = columns_ref[8 * INVERSE : 8 * INVERSE + 8, :]
    along_y, part = column_product(OUTWARD, 0), total * inverse
    stacked = jnp.concatenate(
        [turned[:3], along_y[:3], part[:3], inverse[:3], jnp.zeros((4, LANES), F32)], axis=0
    )

    def message(columns, end):
        at = iota((16, LANES), 1)
        line = iota((16, LANES), 0)
        columns = jnp.where(at < cells_x, columns, 0.0)
        for comp in range(3):
            columns = jnp.where(
                (line == 3 + comp) & (at == cells_x),
                ends[:, end + comp : end + comp + 1],
                columns,
            )
        return columns

    inner_ref[...], outer_ref[...] = by_parity(
        message(stacked, 9), message(pltpu.roll(stacked, cells_x, 1), 0)
    )


def bernstein(coord):
    other = 1.0 - coord
    return [
        other * other * other,
        3.0 * coord * other * other,
        3.0 * coord * coord * other,
        coord * coord * coord,
    ]


def weight_table(u, v, w):
    first, second, third = bernstein(u), bernstein(v), bernstein(w)
    line = iota((8, u.shape[1]), 0)
    inner = line & 3
    along = jnp.where(
        inner == 0,
        third[0],
        jnp.where(inner == 1, third[1], jnp.where(inner == 2, third[2], third[3])),
    )
    pair = jnp.concatenate(
        [
            jnp.where(line < 4, second[0], second[1]) * along,
            jnp.where(line < 4, second[2], second[3]) * along,
        ],
        axis=0,
    )
    return jnp.concatenate([pair * first[i] for i in range(4)], axis=0)


def tile_rows(terms):
    first_half = iota((4, LANES), 1) < LANES // 2
    rows = []
    for term in terms:
        term = term[:8] + term[8:]
        term = term + pltpu.roll(term, LANES // 2, 1)
        rows.append(jnp.where(first_half, term[:4], term[4:]))
    return jnp.concatenate(two_parts(jnp.concatenate(rows, axis=0)), axis=0).astype(BF16)


def box_matrix(tile_row, boxes):
    tiles = tile_row.shape[1]
    shape = (4 * boxes, 8 * tiles)
    column = iota((1, shape[1]), 1)
    box = jnp.zeros((1, shape[1]), jnp.int32)
    for tile in range(tiles):
        mine = lax.rem(lax.shift_right_logical(column, 2), tiles) == tile
        box = jnp.where(mine, tile_row[:, tile : tile + 1], box)
    target = 4 * box + (column & 3)
    return jnp.where(iota(shape, 0) == target, 1.0, 0.0).astype(BF16)


def by_parity(low, high):
    odd = lax.rem(lax.axis_index("gy"), 2) == 1
    return jnp.where(odd, high, low), jnp.where(odd, low, high)


def quotient_before(halo_ref, strip_ref, before_ref, entering):
    def rows(ref, first, count):
        return [ref[first + k : first + k + 1, :] for k in range(count)]

    beside, inverse = rows(halo_ref, 0, 3), rows(halo_ref, 3, 3)
    far_load, within = rows(halo_ref, 18, 3), rows(strip_ref, 0, 6)
    far_scale = rows(strip_ref, 33, 3)
    far = [ratio(far_load[c], far_scale[c]) for c in range(3)]
    whole_block = [None, *within[:3], None, *within[3:], None]
    total = off_diagonal(lambda k: whole_block[k], beside)
    from_far = product(lambda k: strip_ref[24 + k : 25 + k, :], far)
    up_y = product(lambda k: strip_ref[6 + k : 7 + k, :], beside)
    low_y = product(lambda k: strip_ref[15 + k : 16 + k, :], beside)
    for c in range(3):
        before_ref[c : c + 1, :] = inverse[c] * (
            total[c]
            + from_far[c]
            + entering[c]
            + lanes_moved(up_y[c], 0.0, 1)
            + lanes_moved(low_y[c], 0.0, -1)
        )
    before_ref[3:, :] = jnp.zeros((before_ref.shape[0] - 3, LANES), F32)


def box_kernel(
    tile_ref, field_ref, node_ref, param_ref, halo_ref, strip_ref, diag_ref, edge_ref,
    mask_ref, inverse_ref,
    part_ref, box_ref, adjoint_ref, before_ref, matrix_ref, weights_ref, columns_ref,
    *, tile_points,
):
    cells_x = field_ref.shape[1]
    own = cells_x // 2
    field = [field_ref[c] for c in range(3)]
    part = off_diagonal(lambda k: diag_ref[k], field)
    up_x = masked_product(edge_ref, mask_ref, 0, field)
    low_x = masked_product(edge_ref, mask_ref, 1, field)
    up_y = masked_product(edge_ref, mask_ref, 2, field)
    low_y = masked_product(edge_ref, mask_ref, 3, field)
    for c in range(3):
        part[c] = inverse_ref[c] * (
            part[c]
            + rows_moved(up_x[c], halo_ref[6 + c : 7 + c, :], 1)
            + rows_moved(low_x[c], halo_ref[21 + c : 22 + c, :], -1)
            + lanes_moved(up_y[c], 0.0, 1)
            + lanes_moved(low_y[c], 0.0, -1)
        )
        part_ref[c] = part[c]
    quotient_before(halo_ref, strip_ref, before_ref, [p[:1] for p in low_x])
    order = [field[0], part[0], field[2], field[1], part[1], part[2]]
    folded = [two_parts(jnp.concatenate([f[:own], f[own:]], axis=1)) for f in order]
    table = jnp.concatenate(
        [folded[f][which] for which in range(2) for f in range(6)], axis=0
    ).astype(BF16)
    points = param_ref.shape[1]
    pieces = CHUNK // LANES
    zero, one = jnp.zeros((), BF16), jnp.ones((), BF16)
    at_node = float_iota((2 * LANES, CHUNK), 0).astype(BF16)
    nothing = jnp.zeros((1, CHUNK), F32)
    highs, lows = [], []
    for chunk in range(points // CHUNK):
        node = jnp.concatenate(
            [node_ref[chunk * pieces + k : chunk * pieces + k + 1, :] for k in range(pieces)],
            axis=1,
        )
        row = lax.shift_right_logical(node, 7)
        column = node & (LANES - 1)
        lanes = slice(chunk * CHUNK, (chunk + 1) * CHUNK)
        at_edge = jnp.where(
            column == 0, row, jnp.where(column == LANES - 1, row + cells_x, -1)
        ).astype(F32)
        columns_ref[:, lanes] = jnp.where(
            at_node[: 2 * cells_x] == stretched(at_edge, 2 * cells_x), one, zero
        )
        place = column + jnp.where(row >= own, LANES, 0)
        row = jnp.where(row >= own, row - own, row)
        pick = jnp.where(at_node == stretched(place.astype(F32), 2 * LANES), one, zero)
        read = jnp.dot(table, pick, preferred_element_type=F32)
        read = read[: 6 * own] + read[6 * own :]
        here = iota((own, CHUNK), 0) == row
        values = [
            jnp.sum(
                jnp.where(here, read[f * own : (f + 1) * own], 0.0), axis=0, keepdims=True
            )
            for f in range(6)
        ]
        high, low = two_parts(
            jnp.concatenate(values[:3] + [nothing] + values[3:] + [nothing], axis=0)
        )
        highs.append(high)
        lows.append(low)
        weights = two_parts(
            weight_table(param_ref[0:1, lanes], param_ref[1:2, lanes], param_ref[2:3, lanes])
        )
        for k in range(CHUNK // tile_points):
            tile = slice(k * tile_points, (k + 1) * tile_points)
            sides = jnp.concatenate([weights[0][:, tile], weights[1][:, tile]], axis=0)
            weights_ref[chunk * (CHUNK // tile_points) + k] = sides.T.astype(BF16)
    both = jnp.concatenate(
        [jnp.concatenate(highs, axis=1), jnp.concatenate(lows, axis=1)], axis=0
    ).astype(BF16)
    matrix_ref[...] = box_matrix(tile_ref[...], matrix_ref.shape[0] // 4)
    tiles = tile_ref.shape[1]
    terms = [
        jnp.dot(
            both[:, tile * tile_points : (tile + 1) * tile_points],
            weights_ref[tile],
            preferred_element_type=F32,
        )
        for tile in range(tiles)
    ]
    box_ref[...] = jnp.dot(matrix_ref[...], tile_rows(terms), preferred_element_type=F32)
    low_half = iota((2 * cells_x, LANES), 1) < LANES // 2
    for tile in range(tiles):
        lanes = slice(tile * tile_points, (tile + 1) * tile_points)
        term = jnp.dot(
            columns_ref[:, lanes], weights_ref[tile], preferred_element_type=F32
        )
        high, low = two_parts(term + pltpu.roll(term, LANES // 2, 1))
        adjoint_ref[:, tile * LANES : (tile + 1) * LANES] = jnp.where(
            low_half, high, low
        ).astype(BF16)


def sums_kernel(
    from_inner_ref, from_outer_ref, inner_ref, outer_ref, field_ref, part_ref, halo_ref,
    diag_ref, edge_ref, mask_ref, box_ref, adjoint_ref, before_ref, matrix_ref,
    quotient_ref, out_ref,
):
    cells_x = field_ref.shape[1]
    targets = out_ref.shape[0]

    from_low, from_high = by_parity(from_inner_ref[...], from_outer_ref[...])
    first, last = by_parity(inner_ref[...], outer_ref[...])

    lane_row = iota((1, LANES), 1)
    shares, edges = [], []
    for arrived, own in ((from_low, first), (from_high, last)):
        def row(source, slot, c):
            return source[3 * slot + c : 3 * slot + c + 1]

        shares.append([row(arrived, 1, c) * row(own, 3, c) for c in range(3)])
        edges.append(
            [row(arrived, 2, c) + row(arrived, 3, c) * row(own, 1, c) for c in range(3)]
        )

    def turned(columns, share, edge):
        kept = [
            jnp.where(lane_row < cells_x, share[c], columns[3 + c : 4 + c]) for c in range(3)
        ]
        rest = jnp.zeros((LANES - 9, LANES), F32)
        return jnp.concatenate([columns[:3], *kept, *edge, rest], axis=0).T

    low = turned(from_low, shares[0], edges[0])
    high = turned(from_high, shares[1], edges[1])
    lane = iota((cells_x, LANES), 1)

    def column(source, slot, comp):
        return source[:cells_x, 3 * slot + comp : 3 * slot + comp + 1]

    field = [field_ref[c] for c in range(3)]
    scale = [diag_ref[4 * c] for c in range(3)]
    quotient, low_edge, high_edge = [], [], []
    for c in range(3):
        entering = jnp.where(
            lane == 0,
            column(low, 1, c),
            jnp.where(lane == LANES - 1, column(high, 1, c), 0.0),
        )
        quotient.append(part_ref[c] + entering)
        low_edge.append(column(low, 2, c))
        high_edge.append(column(high, 2, c))
    for c in range(3):
        quotient_ref[c] = quotient[c]
    before, before_quotient = [], []
    for c in range(3):
        entering = jnp.where(
            lane_row == 0,
            low[cells_x : cells_x + 1, 3 + c : 4 + c],
            jnp.where(lane_row == LANES - 1, high[cells_x : cells_x + 1, 3 + c : 4 + c], 0.0),
        )
        before.append(halo_ref[c : c + 1, :])
        before_quotient.append(
            before_ref[c : c + 1, :] + entering * halo_ref[3 + c : 4 + c, :]
        )

    first_sum = sum(field[c] * scale[c] * field[c] for c in range(3))
    second_sum = sum(field[c] * scale[c] * quotient[c] for c in range(3))
    third_sum = sum(quotient[c] * scale[c] * quotient[c] for c in range(3))
    within = off_diagonal(lambda k: diag_ref[k], quotient)
    fourth_sum = sum(within[c] * field[c] for c in range(3))
    fifth_sum = sum(within[c] * quotient[c] for c in range(3))
    at_row = iota((cells_x, LANES), 0)
    moves = (
        (pltpu.roll, 1, 0, at_row == 0),
        (pltpu.roll, cells_x - 1, 0, at_row == cells_x - 1),
        (pltpu.roll, 1, 1, lane == 0),
        (pltpu.roll, LANES - 1, 1, lane == LANES - 1),
    )
    extra = [0.0, 0.0]
    sides = [0.0, 0.0]
    for direction, (roll, step, dim, edge) in enumerate(moves):
        moving = masked_product(edge_ref, mask_ref, direction, quotient)
        for c in range(3):
            moved = jnp.where(edge, 0.0, roll(moving[c], step, dim))
            fourth_sum = fourth_sum + moved * field[c]
            fifth_sum = fifth_sum + moved * quotient[c]
            if direction == 1:
                extra[0] += moving[c][:1] * before[c]
                extra[1] += moving[c][:1] * before_quotient[c]
            elif direction == 2:
                sides[0] += moving[c][:, LANES - 1 :] * column(high, 0, c)
                sides[1] += moving[c][:, LANES - 1 :] * high_edge[c]
            elif direction == 3:
                sides[0] += moving[c][:, :1] * column(low, 0, c)
                sides[1] += moving[c][:, :1] * low_edge[c]
    incoming = product(lambda k: halo_ref[9 + k : 10 + k, :], before_quotient)
    extra[0] += sum(incoming[c] * field[c][:1] for c in range(3))
    extra[1] += sum(incoming[c] * quotient[c][:1] for c in range(3))
    fourth_sum = fourth_sum + jnp.where(lane == 0, sides[0], 0.0)
    fifth_sum = fifth_sum + jnp.where(lane == 0, sides[1], 0.0)
    extra = [0.0, 0.0, 0.0, extra[0], extra[1]]
    sums = jnp.zeros((1, LANES), F32)
    for k, value in enumerate((first_sum, second_sum, third_sum, fourth_sum, fifth_sum)):
        line = jnp.sum(value, axis=0, keepdims=True) + extra[k]
        sums = jnp.where(lane_row == k, jnp.sum(line, axis=1, keepdims=True), sums)

    added = [
        jnp.where(lane_row < cells_x, shares[0][c], pltpu.roll(shares[1][c], cells_x, 1))
        for c in range(3)
    ]
    none = jnp.zeros((1, LANES), F32)
    added = jnp.concatenate(
        [none, added[0], none, none, none, added[1], added[2], none], axis=0
    )
    added = jnp.concatenate(two_parts(added), axis=0).astype(BF16)
    terms = jnp.dot(added, adjoint_ref[...], preferred_element_type=F32)
    terms = [
        terms[:, first : first + LANES] for first in range(0, terms.shape[1], LANES)
    ]
    total = box_ref[...] + jnp.dot(
        matrix_ref[...], tile_rows(terms), preferred_element_type=F32
    )
    total = jnp.where((iota(total.shape, 0) & 3) == 3, sums, total)
    for box in range(targets):
        out_ref[box] = total[4 * box : 4 * box + 4]


def result_kernel(got_ref, field_ref, quotient_ref, solution_ref, gradient_ref):
    total = jnp.sum(got_ref[...], axis=0)
    rho, a, b, t, u = [total[3:4, k : k + 1] for k in range(5)]
    norm = rho + a
    by_rho, by_norm = 1.0 / rho, 1.0 / norm
    ratio, step = a * by_rho, rho * by_norm
    rest = jnp.maximum(b - a * ratio, 0.0)
    beta = step * step * rest * by_rho
    rest_image = (b + u) - ratio * (a + b + a + t) + ratio * ratio * norm
    cross = (a + t) - ratio * norm
    curve = step * step * rest_image - step * beta * (rest + cross) + beta * beta * norm
    second = jnp.where(
        curve > 0.0, step * step * rest / jnp.where(curve > 0.0, curve, 1.0), 0.0
    )
    second = jnp.minimum(second, 16.0)
    of_field = step + second * (beta + step * ratio)
    of_quotient = -(step * second)
    for c in range(3):
        solution_ref[c] = of_field * field_ref[c] + of_quotient * quotient_ref[c]
    gradient_ref[:, :LANES] = of_field * total[0:1] + of_quotient * total[1:2]
    gradient_ref[:, LANES:] = (
        of_field * total[2:3, : LANES // 2] + of_quotient * total[2:3, LANES // 2 :]
    )


def per_device(
    diag_blocks, edge_blocks, edge_mask, src_values, src_owner, src_node, src_count,
    surf_node, surf_param, tile_box,
):
    cells_x, cells_y = diag_blocks.shape[1:]
    width_gx, width_gy = lax.axis_size("gx"), lax.axis_size("gy")
    devices = width_gx * width_gy
    groups = src_node.shape[0] // LANES
    whole = functools.partial(jax.ShapeDtypeStruct, dtype=F32)

    cells = 4 * groups + NEAR

    def kept(array):
        return pltpu.with_memory_space_constraint(array, pltpu.HBM)

    i32 = jnp.int32
    rows, strip = pl.pallas_call(
        pack_kernel,
        in_specs=[SMEM] + [HBM] * 6,
        out_specs=[HBM, VMEM],
        out_shape=[
            pltpu.HBM((width_gx, cells, LANES), F32), pltpu.VMEM((STRIP, LANES), F32)
        ],
        scratch_shapes=[
            pltpu.VMEM(src_values.shape, F32),
            pltpu.VMEM((groups, LANES), i32),
            pltpu.VMEM((groups, LANES), i32),
            pltpu.VMEM((9, 8, cells_y), F32),
            pltpu.VMEM((9, 8, cells_y), F32),
            pltpu.VMEM((9, 8, cells_y), F32),
            pltpu.VMEM((4, 9, 8, cells_y), F32),
            pltpu.VMEM((8, cells_y), i32),
            pltpu.VMEM((4, 8, cells_y), i32),
            pltpu.VMEM((width_gx, cells, LANES), F32),
            pltpu.SemaphoreType.DMA((9,)),
            pltpu.SemaphoreType.DMA((2,)),
        ],
        compiler_params=PARAMS,
        name="pack_rows_and_edges",
    )(
        src_count, kept(src_values),
        kept(src_owner.reshape(groups, LANES)), kept(src_node.reshape(groups, LANES)),
        kept(diag_blocks), kept(edge_blocks), kept(edge_mask),
    )
    rows = lax.all_to_all(rows, "gx", split_axis=0, concat_axis=0, tiled=True)
    strip = lax.ppermute(strip, "gx", [(i, i + 1) for i in range(width_gx - 1)])

    nodes = (3, cells_x, cells_y)
    inverse, columns = pl.pallas_call(
        edge_kernel,
        in_specs=[VMEM] * 3,
        out_specs=[VMEM] * 2,
        out_shape=[whole(nodes), whole((LANES, LANES))],
        compiler_params=PARAMS,
        cost_estimate=pl.CostEstimate(
            flops=10**8, bytes_accessed=4 * 10**6, transcendentals=0
        ),
        name="edge_columns",
    )(diag_blocks, edge_blocks, edge_mask)

    size = -(-3 * (cells_x + 2 * PAD) // 16) * 16
    field, halo, inner, outer = pl.pallas_call(
        field_kernel,
        in_specs=[VMEM] * 3,
        out_specs=[VMEM] * 4,
        out_shape=[
            whole(nodes), whole((24, cells_y)), whole((16, LANES)), whole((16, LANES)),
        ],
        scratch_shapes=[pltpu.VMEM((size, 2 * LANES), F32)],
        compiler_params=PARAMS,
        name="load_and_first_product",
    )(rows, inverse, columns)
    def swapped(columns, first):
        low = range(first, width_gy - 1, 2)
        pairs = [(i, i + 1) for i in low] + [(i + 1, i) for i in low]
        return lax.ppermute(columns, "gy", pairs)

    from_inner, from_outer = swapped(inner, 1), swapped(outer, 0)
    points, tiles = surf_node.shape[0], tile_box.shape[0]
    part, box_part, adjoint, before, matrix = pl.pallas_call(
        functools.partial(box_kernel, tile_points=points // tiles),
        in_specs=[VMEM] * 10,
        out_specs=[VMEM] * 5,
        out_shape=[
            whole(nodes),
            whole((4 * devices, LANES)),
            jax.ShapeDtypeStruct((2 * cells_x, tiles * LANES), BF16),
            whole((8, LANES)),
            jax.ShapeDtypeStruct((4 * devices, 8 * tiles), BF16),
        ],
        scratch_shapes=[
            pltpu.VMEM((tiles, points // tiles, LANES), BF16),
            pltpu.VMEM((2 * cells_x, points), BF16),
        ],
        compiler_params=PARAMS,
        cost_estimate=pl.CostEstimate(
            flops=10**9, bytes_accessed=4 * 10**6, transcendentals=0
        ),
        name="box_parts",
    )(
        tile_box.reshape(1, tiles), field, surf_node.reshape(points // LANES, LANES),
        surf_param, halo, strip, diag_blocks, edge_blocks, edge_mask, inverse,
    )

    quotient, partial = pl.pallas_call(
        sums_kernel,
        in_specs=[VMEM] * 14,
        out_specs=[VMEM] * 2,
        out_shape=[whole(nodes), whole((devices, 4, LANES))],
        compiler_params=PARAMS,
        name="sums_and_halo_parts",
    )(
        from_inner, from_outer, inner, outer, field, part, halo, diag_blocks, edge_blocks, edge_mask,
        box_part, adjoint, before, matrix,
    )
    got = lax.all_to_all(partial, ("gx", "gy"), split_axis=0, concat_axis=0, tiled=True)
    return pl.pallas_call(
        result_kernel,
        in_specs=[VMEM] * 3,
        out_specs=[VMEM] * 2,
        out_shape=[whole(nodes), whole((1, 192))],
        compiler_params=PARAMS,
        name="steps_and_outputs",
    )(got, field, quotient)


def solution(mesh):
    return jax.shard_map(
        per_device,
        mesh=mesh,
        in_specs=(
            P(None, "gx", "gy"),
            P(None, None, "gx", "gy"),
            P(None, "gx", "gy"),
            P(None, ("gx", "gy")),
            P(("gx", "gy"), None),
            P(("gx", "gy")),
            P(("gx", "gy")),
            P(("gx", "gy")),
            P(None, ("gx", "gy")),
            P(("gx", "gy")),
        ),
        out_specs=(P(None, "gx", "gy"), P(("gx", "gy"), None)),
        check_vma=False,
    )
```

profile of v0, /device:TPU:0, one launch (start us, length us, event | category | flops | bytes accessed | tf_op | source)
XLA Modules:
  0.0 34.9 jit_solution(11194521221914712495)
XLA Ops:
  0.6 0.0 copy-start.2
  0.6 0.0 copy-start
  0.7 0.0 copy-start.1
  1.4 1.9 %pack_rows_and_edges.1 = (f32[8,48,128]{2,1,0:T(8,128)}, f32[40,128]{1,0:T(8,128)S(1)}) custom-call(s32[1]{0:T(128)S(6)} %copy.12.count_ref, f32[3,1024]{1,0:T(4,128)} %values_in.1, s32[8,128]{1,0:T(8,128)} %bitcast.6, s32[8,128]{1,0:T(8,128)} %bitcast.7, f32[9,64,128]{2,1,0:T(8,128)} %diag_ref.5, f32[4,9,64,128]{3,2,1,0:T(8,128)} %edge_ref.5, ...), custom_call_target="tpu_custom_call" | custom-call | tf_op jit(solution)/shard_map/pack_rows_and_edges/pallas_call | solution.py:742
  3.3 0.0 copy-start.3
  3.3 0.0 copy-start.4
  3.3 0.0 copy-start.5
  3.4 5.3 %all-to-all-start = ((f32[8,48,128]{2,1,0:T(8,128)}), f32[8,48,128]{2,1,0:T(8,128)S(1)}, u32[]{:S(2)}, u32[]{:S(2)}) async-start(f32[8,48,128]{2,1,0:T(8,128)} %get-tuple-element.17), calls=%async_computation | async-start | bytes 393216 | tf_op jit(solution)/shard_map/all_to_all | solution.py:770
  8.7 2.4 %collective-permute-start.2 = (f32[40,128]{1,0:T(8,128)S(1)}, f32[40,128]{1,0:T(8,128)S(1)}, u32[]{:S(2)}, u32[]{:S(2)}) collective-permute-start(f32[40,128]{1,0:T(8,128)S(1)} %get-tuple-element.24), channel_id=1, source_target_pairs={{0,4},{4,8},{8,12},{12,16},{16,20},{20,24},{24,28},{1,5},{5,9},{9,... | collective-permute-start | bytes 61448 | tf_op jit(solution)/shard_map/ppermute | solution.py:771
  11.1 0.0 copy-done.2
  11.1 0.0 copy-done
  11.1 1.1 %edge_columns.1 = (f32[3,64,128]{2,1,0:T(8,128)S(1)}, f32[128,128]{1,0:T(8,128)S(1)}) custom-call(f32[9,64,128]{2,1,0:T(8,128)S(1)} %copy-done.1, f32[4,9,64,128]{3,2,1,0:T(8,128)S(1)} %copy-done, s32[4,64,128]{2,1,0:T(8,128)S(1)} %copy-done.2), custom_call_target="tpu_custom_call" | custom-call | flops 100000000 | bytes 4000000 | tf_op jit(solution)/shard_map/edge_columns/pallas_call | solution.py:774
  12.2 2.7 %all-to-all-done.rows_ref = f32[8,48,128]{2,1,0:T(8,128)S(1)} async-done(((f32[8,48,128]{2,1,0:T(8,128)}), f32[8,48,128]{2,1,0:T(8,128)S(1)}, u32[]{:S(2)}, u32[]{:S(2)}) %all-to-all-start) | async-done | bytes 196640 | tf_op jit(solution)/shard_map/all_to_all | solution.py:770
  14.9 1.9 %load_and_first_product.1 = (f32[3,64,128]{2,1,0:T(8,128)S(1)}, f32[24,128]{1,0:T(8,128)S(1)}, f32[16,128]{1,0:T(8,128)S(1)}, f32[16,128]{1,0:T(8,128)S(1)}) custom-call(f32[8,48,128]{2,1,0:T(8,128)S(1)} %all-to-all-done.rows_ref, f32[3,64,128]{2,1,0:T(8,128)S(1)} %get-tuple-element.18.inverse_ref, f32[128,128]{1,0:T(8,128)S(1)} %get-tuple-element.19.columns_ref), custom_call_target="tpu_custom_call" | custom-call | tf_op jit(solution)/shard_map/load_and_first_product/pallas_call | solution.py:787
  16.8 0.7 %collective-permute-start = (f32[16,128]{1,0:T(8,128)S(1)}, f32[16,128]{1,0:T(8,128)S(1)}, u32[]{:S(2)}, u32[]{:S(2)}) collective-permute-start(f32[16,128]{1,0:T(8,128)S(1)} %get-tuple-element.20.inner_ref), channel_id=1, source_target_pairs={{1,2},{2,1},{5,6},{6,5},{9,10},{10,9},{13,14},{14,13},{17,18},{18,... | collective-permute-start | bytes 24584 | tf_op jit(solution)/shard_map/ppermute | solution.py:801
  17.5 4.5 %collective-permute-start.1 = (f32[16,128]{1,0:T(8,128)S(1)}, f32[16,128]{1,0:T(8,128)S(1)}, u32[]{:S(2)}, u32[]{:S(2)}) collective-permute-start(f32[16,128]{1,0:T(8,128)S(1)} %get-tuple-element.21.outer_ref), channel_id=1, source_target_pairs={{0,1},{2,3},{1,0},{3,2},{4,5},{6,7},{5,4},{7,6},{8,9},{10,11},{9,8... | collective-permute-start | bytes 24584 | tf_op jit(solution)/shard_map/ppermute | solution.py:801
  22.0 0.0 collective-permute-done.2.strip_ref
  22.0 0.0 copy-done.5
  22.0 1.4 %box_parts.1 = (f32[3,64,128]{2,1,0:T(8,128)S(1)}, f32[128,128]{1,0:T(8,128)S(1)}, bf16[128,2048]{1,0:T(8,128)(2,1)S(1)}, f32[8,128]{1,0:T(8,128)S(1)}, bf16[128,128]{1,0:T(8,128)(2,1)S(1)}) custom-call(s32[1,16]{1,0:T(1,128)S(1)} %bitcast.5, f32[3,64,128]{2,1,0:T(8,128)S(1)} %get-tuple-element.22.field_ref, s32[16,128]{1,0:T(8,128)S(1)} %bitcast.4, ...), custom_call_target="tpu_custom_call" | custom-call | flops 1000000000 | bytes 4000000 | tf_op jit(solution)/shard_map/box_parts/pallas_call | solution.py:805
  23.4 0.0 collective-permute-done.from_inner_ref
  23.4 0.1 collective-permute-done.1.from_outer_ref
  23.6 0.6 %sums_and_halo_parts.1 = (f32[3,64,128]{2,1,0:T(8,128)S(1)}, f32[32,4,128]{2,1,0:T(4,128)S(1)}) custom-call(f32[16,128]{1,0:T(8,128)S(1)} %collective-permute-done.from_inner_ref, f32[16,128]{1,0:T(8,128)S(1)} %collective-permute-done.1.from_outer_ref, f32[16,128]{1,0:T(8,128)S(1)} %get-tuple-element.20.inner_ref, ...), custom_call_target="tpu_custom_call" | custom-call | tf_op jit(solution)/shard_map/sums_and_halo_parts/pallas_call | solution.py:830
  24.2 9.7 %all_to_all.10.got_ref = f32[32,4,128]{2,1,0:T(4,128)S(1)} all-to-all(f32[32,4,128]{2,1,0:T(4,128)S(1)} %get-tuple-element.30), channel_id=1, replica_groups=mesh['gx'=8,'gy'=4] {'gx','gy'}, dimensions={0} | all-to-all | bytes 131072 | tf_op jit(solution)/shard_map/all_to_all | solution.py:841
  33.9 1.0 %steps_and_outputs.1 = (f32[3,64,128]{2,1,0:T(8,128)}, f32[1,192]{1,0:T(1,128)}) custom-call(f32[32,4,128]{2,1,0:T(4,128)S(1)} %all_to_all.10.got_ref, f32[3,64,128]{2,1,0:T(8,128)S(1)} %get-tuple-element.22.field_ref, f32[3,64,128]{2,1,0:T(8,128)S(1)} %get-tuple-element.31.quotient_ref), custom_call_target="tpu_custom_call" | custom-call | tf_op jit(solution)/shard_map/steps_and_outputs/pallas_call | solution.py:842
  (3 shorter events, 0.0 us)
Async XLA Ops:
  0.6 10.5 %copy-start.2 = (s32[4,64,128]{2,1,0:T(8,128)S(1)}, s32[4,64,128]{2,1,0:T(8,128)}, u32[]{:S(2)}) copy-start(s32[4,64,128]{2,1,0:T(8,128)} %mask_ref.5) | copy-start | bytes 393220
  0.6 10.5 %copy-start = (f32[4,9,64,128]{3,2,1,0:T(8,128)S(1)}, f32[4,9,64,128]{3,2,1,0:T(8,128)}, u32[]{:S(2)}) copy-start(f32[4,9,64,128]{3,2,1,0:T(8,128)} %edge_ref.5) | copy-start | bytes 3538948
  0.7 10.5 %copy-start.1 = (f32[9,64,128]{2,1,0:T(8,128)S(1)}, f32[9,64,128]{2,1,0:T(8,128)}, u32[]{:S(2)}) copy-start(f32[9,64,128]{2,1,0:T(8,128)} %diag_ref.5) | copy-start | bytes 884740
  3.3 18.6 %copy-start.3 = (f32[3,2048]{1,0:T(4,128)S(1)}, f32[3,2048]{1,0:T(4,128)}, u32[]{:S(2)}) copy-start(f32[3,2048]{1,0:T(4,128)} %param_ref.1) | copy-start | bytes 73732
  3.3 18.6 %copy-start.4 = (s32[2048]{0:T(1024)S(1)}, s32[2048]{0:T(1024)}, u32[]{:S(2)}) copy-start(s32[2048]{0:T(1024)} %param.17) | copy-start | bytes 24580
  3.3 18.6 %copy-start.5 = (s32[16]{0:T(128)S(1)}, s32[16]{0:T(128)}, u32[]{:S(2)}) copy-start(s32[16]{0:T(128)} %param.19) | copy-start | bytes 196
  3.4 11.6 %all-to-all-start = ((f32[8,48,128]{2,1,0:T(8,128)}), f32[8,48,128]{2,1,0:T(8,128)S(1)}, u32[]{:S(2)}, u32[]{:S(2)}) async-start(f32[8,48,128]{2,1,0:T(8,128)} %get-tuple-element.17), calls=%async_computation | async-start | bytes 393216 | tf_op jit(solution)/shard_map/all_to_all | solution.py:770
  8.7 13.3 %collective-permute-start.2 = (f32[40,128]{1,0:T(8,128)S(1)}, f32[40,128]{1,0:T(8,128)S(1)}, u32[]{:S(2)}, u32[]{:S(2)}) collective-permute-start(f32[40,128]{1,0:T(8,128)S(1)} %get-tuple-element.24), channel_id=1, source_target_pairs={{0,4},{4,8},{8,12},{12,16},{16,20},{20,24},{24,28},{1,5},{5,9},{9,... | collective-permute-start | bytes 61448 | tf_op jit(solution)/shard_map/ppermute | solution.py:771
  16.8 6.6 %collective-permute-start = (f32[16,128]{1,0:T(8,128)S(1)}, f32[16,128]{1,0:T(8,128)S(1)}, u32[]{:S(2)}, u32[]{:S(2)}) collective-permute-start(f32[16,128]{1,0:T(8,128)S(1)} %get-tuple-element.20.inner_ref), channel_id=1, source_target_pairs={{1,2},{2,1},{5,6},{6,5},{9,10},{10,9},{13,14},{14,13},{17,18},{18,... | collective-permute-start | bytes 24584 | tf_op jit(solution)/shard_map/ppermute | solution.py:801
  17.5 6.1 %collective-permute-start.1 = (f32[16,128]{1,0:T(8,128)S(1)}, f32[16,128]{1,0:T(8,128)S(1)}, u32[]{:S(2)}, u32[]{:S(2)}) collective-permute-start(f32[16,128]{1,0:T(8,128)S(1)} %get-tuple-element.21.outer_ref), channel_id=1, source_target_pairs={{0,1},{2,3},{1,0},{3,2},{4,5},{6,7},{5,4},{7,6},{8,9},{10,11},{9,8... | collective-permute-start | bytes 24584 | tf_op jit(solution)/shard_map/ppermute | solution.py:801
where the time goes:
time: 35.3 us; the launch traced here: 34.9 us
  starting transfers between devices  12.8 us (36%)
  blocking collectives  9.69 us (27%)
  Pallas kernels  8.01 us (23%)
  waiting for transfers between devices  2.85 us (8%)
  between operations  1.52 us (4%)
    all_to_all x1, blocking collectives, per_device(): lax.all_to_all(partial, ('gx', 'gy'), split_axis=0, concat_axis=0, tiled=...  9.69 us
    all_to_all x1, starting transfers between devices, per_device(): rows = lax.all_to_all(rows, 'gx', split_axis=0, concat_axis=0, tiled=True)  5.32 us
    ppermute x2, starting transfers between devices, swapped(): return lax.ppermute(columns, 'gy', pairs)  5.12 us
    all_to_all x1, waiting for transfers between devices, per_device(): rows = lax.all_to_all(rows, 'gx', split_axis=0, concat_axis=0, tiled=True)  2.7 us
    ppermute x1, starting transfers between devices, per_device(): strip = lax.ppermute(strip, 'gx', [(i, i + 1) for i in range(width_gx - 1)])  2.4 us
    pallas_call x1, Pallas kernels, per_device(): pl.pallas_call(field_kernel, in_specs=[VMEM] * 3, out_specs=[VMEM] * 4, o...  1.91 us
    pallas_call x1, Pallas kernels, per_device(): pl.pallas_call(pack_kernel, in_specs=[SMEM] + [HBM] * 6, out_specs=[HBM,...  1.89 us
    pallas_call x1, Pallas kernels, per_device(): pl.pallas_call(functools.partial(box_kernel, tile_points=points // tiles)...  1.45 us
  transfers between devices with their start and end apart: 4, of which 2 were waited for; matrix products, arithmetic and copies ran while one was open for 0% of the time, Pallas kernels for 13%

commit v1 on v0

--- a/solution.py
+++ b/solution.py
@@ -235,7 +235,7 @@
     line = iota((size, LANES), 0)
     block = sum(jnp.where(line >= half * k, 1, 0) for k in range(1, 6))
     at_row = jnp.where(line < 6 * half, line - half * block, -5).astype(F32).astype(BF16)
-    at_column = float_iota((2 * LANES, LANES), 0).astype(BF16)
+    at_column = float_iota((LANES, 2 * LANES), 1).astype(BF16)
     in_tile = float_iota((16, LANES), 0).astype(BF16)
     zero, one = jnp.zeros((), BF16), jnp.ones((), BF16)
 
@@ -251,7 +251,7 @@
         parts = [
             two_parts(rows_ref[sender, c * groups : (c + 1) * groups, :]) for c in range(3)
         ]
-        lefts, rights = [], []
+        lefts = []
         for group in range(groups):
             line = slice(group, group + 1)
             values = [
@@ -269,23 +269,26 @@
                 )
             match = at_row == stretched(place[line], size)
             lefts.append(jnp.where(match, jnp.concatenate(tiles, axis=0), zero))
-            rights.append(
-                jnp.where(at_column == stretched(column[line], 2 * LANES), one, zero)
-            )
-        return lefts, rights
+        return lefts, column
 
     together = math.gcd(senders, 4)
 
     def add_rows(step, carry):
-        lefts, rights = [], []
+        lefts, columns = [], []
         for k in range(together):
-            left, right = operands(step * together + k)
+            left, column = operands(step * together + k)
             lefts += left
-            rights += right
-        load_ref[...] += lax.dot_general(
+            columns.append(column)
+        columns.append(jnp.zeros((LANES - together * groups, LANES), F32))
+        columns = jnp.concatenate(columns, axis=0).T
+        rights = []
+        for k in range(together * groups):
+            column = jnp.broadcast_to(columns[:, k : k + 1], (LANES, LANES)).astype(BF16)
+            column = jnp.concatenate([column, column], axis=1)
+            rights.append(jnp.where(at_column == column, one, zero))
+        load_ref[...] += jnp.dot(
             jnp.concatenate(lefts, axis=1),
-            jnp.concatenate(rights, axis=1),
-            (((1,), (1,)), ((), ())),
+            jnp.concatenate(rights, axis=0),
             preferred_element_type=F32,
         )
         return carry

time: 35.3 us -> 35.4 us (level)
  no operation moved by 1% of the time
where the time goes in v1:
time: 35.4 us; the launch traced here: 35 us
  starting transfers between devices  12.8 us (36%)
  blocking collectives  9.69 us (27%)
  Pallas kernels  8.08 us (23%)
  waiting for transfers between devices  2.85 us (8%)
  between operations  1.52 us (4%)
    all_to_all x1, blocking collectives, per_device(): lax.all_to_all(partial, ('gx', 'gy'), split_axis=0, concat_axis=0, tiled=...  9.69 us
    all_to_all x1, starting transfers between devices, per_device(): rows = lax.all_to_all(rows, 'gx', split_axis=0, concat_axis=0, tiled=True)  5.32 us
    ppermute x2, starting transfers between devices, swapped(): return lax.ppermute(columns, 'gy', pairs)  5.12 us
    all_to_all x1, waiting for transfers between devices, per_device(): rows = lax.all_to_all(rows, 'gx', split_axis=0, concat_axis=0, tiled=True)  2.7 us
    ppermute x1, starting transfers between devices, per_device(): strip = lax.ppermute(strip, 'gx', [(i, i + 1) for i in range(width_gx - 1)])  2.4 us
    pallas_call x1, Pallas kernels, per_device(): pl.pallas_call(field_kernel, in_specs=[VMEM] * 3, out_specs=[VMEM] * 4, o...  1.99 us
    pallas_call x1, Pallas kernels, per_device(): pl.pallas_call(pack_kernel, in_specs=[SMEM] + [HBM] * 6, out_specs=[HBM,...  1.89 us
    pallas_call x1, Pallas kernels, per_device(): pl.pallas_call(functools.partial(box_kernel, tile_points=points // tiles)...  1.45 us
  transfers between devices with their start and end apart: 4, of which 2 were waited for; matrix products, arithmetic and copies ran while one was open for 0% of the time, Pallas kernels for 13%

profile of v1, /device:TPU:0, one launch (start us, length us, event | category | flops | bytes accessed | tf_op | source)
XLA Modules:
  0.0 35.0 jit_solution(17673913953193196813)
XLA Ops:
  0.6 0.0 copy-start.2
  0.6 0.0 copy-start
  0.7 0.0 copy-start.1
  1.4 1.9 %pack_rows_and_edges.1 = (f32[8,48,128]{2,1,0:T(8,128)}, f32[40,128]{1,0:T(8,128)S(1)}) custom-call(s32[1]{0:T(128)S(6)} %copy.12.count_ref, f32[3,1024]{1,0:T(4,128)} %values_in.1, s32[8,128]{1,0:T(8,128)} %bitcast.6, s32[8,128]{1,0:T(8,128)} %bitcast.7, f32[9,64,128]{2,1,0:T(8,128)} %diag_ref.5, f32[4,9,64,128]{3,2,1,0:T(8,128)} %edge_ref.5, ...), custom_call_target="tpu_custom_call" | custom-call | tf_op jit(solution)/shard_map/pack_rows_and_edges/pallas_call | solution.py:745
  3.3 0.0 copy-start.3
  3.3 0.0 copy-start.4
  3.3 0.0 copy-start.5
  3.4 5.3 %all-to-all-start = ((f32[8,48,128]{2,1,0:T(8,128)}), f32[8,48,128]{2,1,0:T(8,128)S(1)}, u32[]{:S(2)}, u32[]{:S(2)}) async-start(f32[8,48,128]{2,1,0:T(8,128)} %get-tuple-element.17), calls=%async_computation | async-start | bytes 393216 | tf_op jit(solution)/shard_map/all_to_all | solution.py:773
  8.7 2.4 %collective-permute-start.2 = (f32[40,128]{1,0:T(8,128)S(1)}, f32[40,128]{1,0:T(8,128)S(1)}, u32[]{:S(2)}, u32[]{:S(2)}) collective-permute-start(f32[40,128]{1,0:T(8,128)S(1)} %get-tuple-element.24), channel_id=1, source_target_pairs={{0,4},{4,8},{8,12},{12,16},{16,20},{20,24},{24,28},{1,5},{5,9},{9,... | collective-permute-start | bytes 61448 | tf_op jit(solution)/shard_map/ppermute | solution.py:774
  11.1 0.0 copy-done.2
  11.1 0.0 copy-done
  11.1 1.1 %edge_columns.1 = (f32[3,64,128]{2,1,0:T(8,128)S(1)}, f32[128,128]{1,0:T(8,128)S(1)}) custom-call(f32[9,64,128]{2,1,0:T(8,128)S(1)} %copy-done.1, f32[4,9,64,128]{3,2,1,0:T(8,128)S(1)} %copy-done, s32[4,64,128]{2,1,0:T(8,128)S(1)} %copy-done.2), custom_call_target="tpu_custom_call" | custom-call | flops 100000000 | bytes 4000000 | tf_op jit(solution)/shard_map/edge_columns/pallas_call | solution.py:777
  12.2 2.7 %all-to-all-done.rows_ref = f32[8,48,128]{2,1,0:T(8,128)S(1)} async-done(((f32[8,48,128]{2,1,0:T(8,128)}), f32[8,48,128]{2,1,0:T(8,128)S(1)}, u32[]{:S(2)}, u32[]{:S(2)}) %all-to-all-start) | async-done | bytes 196640 | tf_op jit(solution)/shard_map/all_to_all | solution.py:773
  14.9 2.0 %load_and_first_product.1 = (f32[3,64,128]{2,1,0:T(8,128)S(1)}, f32[24,128]{1,0:T(8,128)S(1)}, f32[16,128]{1,0:T(8,128)S(1)}, f32[16,128]{1,0:T(8,128)S(1)}) custom-call(f32[8,48,128]{2,1,0:T(8,128)S(1)} %all-to-all-done.rows_ref, f32[3,64,128]{2,1,0:T(8,128)S(1)} %get-tuple-element.18.inverse_ref, f32[128,128]{1,0:T(8,128)S(1)} %get-tuple-element.19.columns_ref), custom_call_target="tpu_custom_call" | custom-call | tf_op jit(solution)/shard_map/load_and_first_product/pallas_call | solution.py:790
  16.9 0.7 %collective-permute-start = (f32[16,128]{1,0:T(8,128)S(1)}, f32[16,128]{1,0:T(8,128)S(1)}, u32[]{:S(2)}, u32[]{:S(2)}) collective-permute-start(f32[16,128]{1,0:T(8,128)S(1)} %get-tuple-element.20.inner_ref), channel_id=1, source_target_pairs={{1,2},{2,1},{5,6},{6,5},{9,10},{10,9},{13,14},{14,13},{17,18},{18,... | collective-permute-start | bytes 24584 | tf_op jit(solution)/shard_map/ppermute | solution.py:804
  17.6 4.5 %collective-permute-start.1 = (f32[16,128]{1,0:T(8,128)S(1)}, f32[16,128]{1,0:T(8,128)S(1)}, u32[]{:S(2)}, u32[]{:S(2)}) collective-permute-start(f32[16,128]{1,0:T(8,128)S(1)} %get-tuple-element.21.outer_ref), channel_id=1, source_target_pairs={{0,1},{2,3},{1,0},{3,2},{4,5},{6,7},{5,4},{7,6},{8,9},{10,11},{9,8... | collective-permute-start | bytes 24584 | tf_op jit(solution)/shard_map/ppermute | solution.py:804
  22.0 0.0 collective-permute-done.2.strip_ref
  22.0 0.0 copy-done.3
  22.0 1.4 %box_parts.1 = (f32[3,64,128]{2,1,0:T(8,128)S(1)}, f32[128,128]{1,0:T(8,128)S(1)}, bf16[128,2048]{1,0:T(8,128)(2,1)S(1)}, f32[8,128]{1,0:T(8,128)S(1)}, bf16[128,128]{1,0:T(8,128)(2,1)S(1)}) custom-call(s32[1,16]{1,0:T(1,128)S(1)} %bitcast.5, f32[3,64,128]{2,1,0:T(8,128)S(1)} %get-tuple-element.22.field_ref, s32[16,128]{1,0:T(8,128)S(1)} %bitcast.4, ...), custom_call_target="tpu_custom_call" | custom-call | flops 1000000000 | bytes 4000000 | tf_op jit(solution)/shard_map/box_parts/pallas_call | solution.py:808
  23.5 0.0 collective-permute-done.from_inner_ref
  23.5 0.1 collective-permute-done.1.from_outer_ref
  23.7 0.6 %sums_and_halo_parts.1 = (f32[3,64,128]{2,1,0:T(8,128)S(1)}, f32[32,4,128]{2,1,0:T(4,128)S(1)}) custom-call(f32[16,128]{1,0:T(8,128)S(1)} %collective-permute-done.from_inner_ref, f32[16,128]{1,0:T(8,128)S(1)} %collective-permute-done.1.from_outer_ref, f32[16,128]{1,0:T(8,128)S(1)} %get-tuple-element.20.inner_ref, ...), custom_call_target="tpu_custom_call" | custom-call | tf_op jit(solution)/shard_map/sums_and_halo_parts/pallas_call | solution.py:833
  24.3 9.7 %all_to_all.10.got_ref = f32[32,4,128]{2,1,0:T(4,128)S(1)} all-to-all(f32[32,4,128]{2,1,0:T(4,128)S(1)} %get-tuple-element.30), channel_id=1, replica_groups=mesh['gx'=8,'gy'=4] {'gx','gy'}, dimensions={0} | all-to-all | bytes 131072 | tf_op jit(solution)/shard_map/all_to_all | solution.py:844
  34.0 1.0 %steps_and_outputs.1 = (f32[3,64,128]{2,1,0:T(8,128)}, f32[1,192]{1,0:T(1,128)}) custom-call(f32[32,4,128]{2,1,0:T(4,128)S(1)} %all_to_all.10.got_ref, f32[3,64,128]{2,1,0:T(8,128)S(1)} %get-tuple-element.22.field_ref, f32[3,64,128]{2,1,0:T(8,128)S(1)} %get-tuple-element.31.quotient_ref), custom_call_target="tpu_custom_call" | custom-call | tf_op jit(solution)/shard_map/steps_and_outputs/pallas_call | solution.py:845
  (3 shorter events, 0.0 us)
Async XLA Ops:
  0.6 10.5 %copy-start.2 = (s32[4,64,128]{2,1,0:T(8,128)S(1)}, s32[4,64,128]{2,1,0:T(8,128)}, u32[]{:S(2)}) copy-start(s32[4,64,128]{2,1,0:T(8,128)} %mask_ref.5) | copy-start | bytes 393220
  0.6 10.5 %copy-start = (f32[4,9,64,128]{3,2,1,0:T(8,128)S(1)}, f32[4,9,64,128]{3,2,1,0:T(8,128)}, u32[]{:S(2)}) copy-start(f32[4,9,64,128]{3,2,1,0:T(8,128)} %edge_ref.5) | copy-start | bytes 3538948
  0.7 10.5 %copy-start.1 = (f32[9,64,128]{2,1,0:T(8,128)S(1)}, f32[9,64,128]{2,1,0:T(8,128)}, u32[]{:S(2)}) copy-start(f32[9,64,128]{2,1,0:T(8,128)} %diag_ref.5) | copy-start | bytes 884740
  3.3 18.7 %copy-start.3 = (f32[3,2048]{1,0:T(4,128)S(1)}, f32[3,2048]{1,0:T(4,128)}, u32[]{:S(2)}) copy-start(f32[3,2048]{1,0:T(4,128)} %param_ref.1) | copy-start | bytes 73732
  3.3 18.7 %copy-start.4 = (s32[2048]{0:T(1024)S(1)}, s32[2048]{0:T(1024)}, u32[]{:S(2)}) copy-start(s32[2048]{0:T(1024)} %param.17) | copy-start | bytes 24580
  3.3 18.7 %copy-start.5 = (s32[16]{0:T(128)S(1)}, s32[16]{0:T(128)}, u32[]{:S(2)}) copy-start(s32[16]{0:T(128)} %param.19) | copy-start | bytes 196
  3.4 11.6 %all-to-all-start = ((f32[8,48,128]{2,1,0:T(8,128)}), f32[8,48,128]{2,1,0:T(8,128)S(1)}, u32[]{:S(2)}, u32[]{:S(2)}) async-start(f32[8,48,128]{2,1,0:T(8,128)} %get-tuple-element.17), calls=%async_computation | async-start | bytes 393216 | tf_op jit(solution)/shard_map/all_to_all | solution.py:773
  8.7 13.3 %collective-permute-start.2 = (f32[40,128]{1,0:T(8,128)S(1)}, f32[40,128]{1,0:T(8,128)S(1)}, u32[]{:S(2)}, u32[]{:S(2)}) collective-permute-start(f32[40,128]{1,0:T(8,128)S(1)} %get-tuple-element.24), channel_id=1, source_target_pairs={{0,4},{4,8},{8,12},{12,16},{16,20},{20,24},{24,28},{1,5},{5,9},{9,... | collective-permute-start | bytes 61448 | tf_op jit(solution)/shard_map/ppermute | solution.py:774
  16.9 6.6 %collective-permute-start = (f32[16,128]{1,0:T(8,128)S(1)}, f32[16,128]{1,0:T(8,128)S(1)}, u32[]{:S(2)}, u32[]{:S(2)}) collective-permute-start(f32[16,128]{1,0:T(8,128)S(1)} %get-tuple-element.20.inner_ref), channel_id=1, source_target_pairs={{1,2},{2,1},{5,6},{6,5},{9,10},{10,9},{13,14},{14,13},{17,18},{18,... | collective-permute-start | bytes 24584 | tf_op jit(solution)/shard_map/ppermute | solution.py:804
  17.6 6.1 %collective-permute-start.1 = (f32[16,128]{1,0:T(8,128)S(1)}, f32[16,128]{1,0:T(8,128)S(1)}, u32[]{:S(2)}, u32[]{:S(2)}) collective-permute-start(f32[16,128]{1,0:T(8,128)S(1)} %get-tuple-element.21.outer_ref), channel_id=1, source_target_pairs={{0,1},{2,3},{1,0},{3,2},{4,5},{6,7},{5,4},{7,6},{8,9},{10,11},{9,8... | collective-permute-start | bytes 24584 | tf_op jit(solution)/shard_map/ppermute | solution.py:804

commit v2 on v0

--- a/solution.py
+++ b/solution.py
@@ -239,6 +239,9 @@
     in_tile = float_iota((16, LANES), 0).astype(BF16)
     zero, one = jnp.zeros((), BF16), jnp.ones((), BF16)
 
+    def one_hot(difference):
+        return jnp.maximum(one - difference * difference, zero)
+
     def operands(sender):
         index = rows_ref[sender, 3 * groups : 4 * groups, :]
         split = float(half * LANES)
@@ -267,11 +270,9 @@
                         in_tile < float(half * high - first), values[low], values[high]
                     )
                 )
-            match = at_row == stretched(place[line], size)
-            lefts.append(jnp.where(match, jnp.concatenate(tiles, axis=0), zero))
-            rights.append(
-                jnp.where(at_column == stretched(column[line], 2 * LANES), one, zero)
-            )
+            match = one_hot(at_row - stretched(place[line], size))
+            lefts.append(match * jnp.concatenate(tiles, axis=0))
+            rights.append(one_hot(at_column - stretched(column[line], 2 * LANES)))
         return lefts, rights
 
     together = math.gcd(senders, 4)

time: 35.3 us -> 35.3 us (level)
  no operation moved by 1% of the time
where the time goes in v2:
time: 35.3 us; the launch traced here: 34.9 us
  starting transfers between devices  12.8 us (36%)
  blocking collectives  9.69 us (27%)
  Pallas kernels  7.99 us (23%)
  waiting for transfers between devices  2.85 us (8%)
  between operations  1.52 us (4%)
    all_to_all x1, blocking collectives, per_device(): lax.all_to_all(partial, ('gx', 'gy'), split_axis=0, concat_axis=0, tiled=...  9.69 us
    all_to_all x1, starting transfers between devices, per_device(): rows = lax.all_to_all(rows, 'gx', split_axis=0, concat_axis=0, tiled=True)  5.32 us
    ppermute x2, starting transfers between devices, swapped(): return lax.ppermute(columns, 'gy', pairs)  5.12 us
    all_to_all x1, waiting for transfers between devices, per_device(): rows = lax.all_to_all(rows, 'gx', split_axis=0, concat_axis=0, tiled=True)  2.7 us
    ppermute x1, starting transfers between devices, per_device(): strip = lax.ppermute(strip, 'gx', [(i, i + 1) for i in range(width_gx - 1)])  2.4 us
    pallas_call x1, Pallas kernels, per_device(): pl.pallas_call(field_kernel, in_specs=[VMEM] * 3, out_specs=[VMEM] * 4, o...  1.9 us
    pallas_call x1, Pallas kernels, per_device(): pl.pallas_call(pack_kernel, in_specs=[SMEM] + [HBM] * 6, out_specs=[HBM,...  1.89 us
    pallas_call x1, Pallas kernels, per_device(): pl.pallas_call(functools.partial(box_kernel, tile_points=points // tiles)...  1.44 us
  transfers between devices with their start and end apart: 4, of which 2 were waited for; matrix products, arithmetic and copies ran while one was open for 0% of the time, Pallas kernels for 13%

profile of v2, /device:TPU:0, one launch (start us, length us, event | category | flops | bytes accessed | tf_op | source)
XLA Modules:
  0.0 34.9 jit_solution(3643215910243862882)
XLA Ops:
  0.6 0.0 copy-start.2
  0.6 0.0 copy-start
  0.7 0.0 copy-start.1
  1.4 1.9 %pack_rows_and_edges.1 = (f32[8,48,128]{2,1,0:T(8,128)}, f32[40,128]{1,0:T(8,128)S(1)}) custom-call(s32[1]{0:T(128)S(6)} %copy.12.count_ref, f32[3,1024]{1,0:T(4,128)} %values_in.1, s32[8,128]{1,0:T(8,128)} %bitcast.6, s32[8,128]{1,0:T(8,128)} %bitcast.7, f32[9,64,128]{2,1,0:T(8,128)} %diag_ref.5, f32[4,9,64,128]{3,2,1,0:T(8,128)} %edge_ref.5, ...), custom_call_target="tpu_custom_call" | custom-call | tf_op jit(solution)/shard_map/pack_rows_and_edges/pallas_call | solution.py:743
  3.3 0.0 copy-start.3
  3.3 0.0 copy-start.4
  3.3 0.0 copy-start.5
  3.4 5.3 %all-to-all-start = ((f32[8,48,128]{2,1,0:T(8,128)}), f32[8,48,128]{2,1,0:T(8,128)S(1)}, u32[]{:S(2)}, u32[]{:S(2)}) async-start(f32[8,48,128]{2,1,0:T(8,128)} %get-tuple-element.17), calls=%async_computation | async-start | bytes 393216 | tf_op jit(solution)/shard_map/all_to_all | solution.py:771
  8.7 2.4 %collective-permute-start.2 = (f32[40,128]{1,0:T(8,128)S(1)}, f32[40,128]{1,0:T(8,128)S(1)}, u32[]{:S(2)}, u32[]{:S(2)}) collective-permute-start(f32[40,128]{1,0:T(8,128)S(1)} %get-tuple-element.24), channel_id=1, source_target_pairs={{0,4},{4,8},{8,12},{12,16},{16,20},{20,24},{24,28},{1,5},{5,9},{9,... | collective-permute-start | bytes 61448 | tf_op jit(solution)/shard_map/ppermute | solution.py:772
  11.1 0.0 copy-done.2
  11.1 0.0 copy-done
  11.1 1.1 %edge_columns.1 = (f32[3,64,128]{2,1,0:T(8,128)S(1)}, f32[128,128]{1,0:T(8,128)S(1)}) custom-call(f32[9,64,128]{2,1,0:T(8,128)S(1)} %copy-done.1, f32[4,9,64,128]{3,2,1,0:T(8,128)S(1)} %copy-done, s32[4,64,128]{2,1,0:T(8,128)S(1)} %copy-done.2), custom_call_target="tpu_custom_call" | custom-call | flops 100000000 | bytes 4000000 | tf_op jit(solution)/shard_map/edge_columns/pallas_call | solution.py:775
  12.2 2.7 %all-to-all-done.rows_ref = f32[8,48,128]{2,1,0:T(8,128)S(1)} async-done(((f32[8,48,128]{2,1,0:T(8,128)}), f32[8,48,128]{2,1,0:T(8,128)S(1)}, u32[]{:S(2)}, u32[]{:S(2)}) %all-to-all-start) | async-done | bytes 196640 | tf_op jit(solution)/shard_map/all_to_all | solution.py:771
  14.9 1.9 %load_and_first_product.1 = (f32[3,64,128]{2,1,0:T(8,128)S(1)}, f32[24,128]{1,0:T(8,128)S(1)}, f32[16,128]{1,0:T(8,128)S(1)}, f32[16,128]{1,0:T(8,128)S(1)}) custom-call(f32[8,48,128]{2,1,0:T(8,128)S(1)} %all-to-all-done.rows_ref, f32[3,64,128]{2,1,0:T(8,128)S(1)} %get-tuple-element.18.inverse_ref, f32[128,128]{1,0:T(8,128)S(1)} %get-tuple-element.19.columns_ref), custom_call_target="tpu_custom_call" | custom-call | tf_op jit(solution)/shard_map/load_and_first_product/pallas_call | solution.py:788
  16.8 0.7 %collective-permute-start = (f32[16,128]{1,0:T(8,128)S(1)}, f32[16,128]{1,0:T(8,128)S(1)}, u32[]{:S(2)}, u32[]{:S(2)}) collective-permute-start(f32[16,128]{1,0:T(8,128)S(1)} %get-tuple-element.20.inner_ref), channel_id=1, source_target_pairs={{1,2},{2,1},{5,6},{6,5},{9,10},{10,9},{13,14},{14,13},{17,18},{18,... | collective-permute-start | bytes 24584 | tf_op jit(solution)/shard_map/ppermute | solution.py:802
  17.5 4.5 %collective-permute-start.1 = (f32[16,128]{1,0:T(8,128)S(1)}, f32[16,128]{1,0:T(8,128)S(1)}, u32[]{:S(2)}, u32[]{:S(2)}) collective-permute-start(f32[16,128]{1,0:T(8,128)S(1)} %get-tuple-element.21.outer_ref), channel_id=1, source_target_pairs={{0,1},{2,3},{1,0},{3,2},{4,5},{6,7},{5,4},{7,6},{8,9},{10,11},{9,8... | collective-permute-start | bytes 24584 | tf_op jit(solution)/shard_map/ppermute | solution.py:802
  21.9 0.0 collective-permute-done.2.strip_ref
  21.9 0.0 copy-done.3
  22.0 1.4 %box_parts.1 = (f32[3,64,128]{2,1,0:T(8,128)S(1)}, f32[128,128]{1,0:T(8,128)S(1)}, bf16[128,2048]{1,0:T(8,128)(2,1)S(1)}, f32[8,128]{1,0:T(8,128)S(1)}, bf16[128,128]{1,0:T(8,128)(2,1)S(1)}) custom-call(s32[1,16]{1,0:T(1,128)S(1)} %bitcast.5, f32[3,64,128]{2,1,0:T(8,128)S(1)} %get-tuple-element.22.field_ref, s32[16,128]{1,0:T(8,128)S(1)} %bitcast.4, ...), custom_call_target="tpu_custom_call" | custom-call | flops 1000000000 | bytes 4000000 | tf_op jit(solution)/shard_map/box_parts/pallas_call | solution.py:806
  23.4 0.0 collective-permute-done.from_inner_ref
  23.4 0.1 collective-permute-done.1.from_outer_ref
  23.6 0.6 %sums_and_halo_parts.1 = (f32[3,64,128]{2,1,0:T(8,128)S(1)}, f32[32,4,128]{2,1,0:T(4,128)S(1)}) custom-call(f32[16,128]{1,0:T(8,128)S(1)} %collective-permute-done.from_inner_ref, f32[16,128]{1,0:T(8,128)S(1)} %collective-permute-done.1.from_outer_ref, f32[16,128]{1,0:T(8,128)S(1)} %get-tuple-element.20.inner_ref, ...), custom_call_target="tpu_custom_call" | custom-call | tf_op jit(solution)/shard_map/sums_and_halo_parts/pallas_call | solution.py:831
  24.2 9.7 %all_to_all.10.got_ref = f32[32,4,128]{2,1,0:T(4,128)S(1)} all-to-all(f32[32,4,128]{2,1,0:T(4,128)S(1)} %get-tuple-element.30), channel_id=1, replica_groups=mesh['gx'=8,'gy'=4] {'gx','gy'}, dimensions={0} | all-to-all | bytes 131072 | tf_op jit(solution)/shard_map/all_to_all | solution.py:842
  33.9 1.0 %steps_and_outputs.1 = (f32[3,64,128]{2,1,0:T(8,128)}, f32[1,192]{1,0:T(1,128)}) custom-call(f32[32,4,128]{2,1,0:T(4,128)S(1)} %all_to_all.10.got_ref, f32[3,64,128]{2,1,0:T(8,128)S(1)} %get-tuple-element.22.field_ref, f32[3,64,128]{2,1,0:T(8,128)S(1)} %get-tuple-element.31.quotient_ref), custom_call_target="tpu_custom_call" | custom-call | tf_op jit(solution)/shard_map/steps_and_outputs/pallas_call | solution.py:843
  (3 shorter events, 0.0 us)
Async XLA Ops:
  0.6 10.5 %copy-start.2 = (s32[4,64,128]{2,1,0:T(8,128)S(1)}, s32[4,64,128]{2,1,0:T(8,128)}, u32[]{:S(2)}) copy-start(s32[4,64,128]{2,1,0:T(8,128)} %mask_ref.5) | copy-start | bytes 393220
  0.6 10.5 %copy-start = (f32[4,9,64,128]{3,2,1,0:T(8,128)S(1)}, f32[4,9,64,128]{3,2,1,0:T(8,128)}, u32[]{:S(2)}) copy-start(f32[4,9,64,128]{3,2,1,0:T(8,128)} %edge_ref.5) | copy-start | bytes 3538948
  0.7 10.5 %copy-start.1 = (f32[9,64,128]{2,1,0:T(8,128)S(1)}, f32[9,64,128]{2,1,0:T(8,128)}, u32[]{:S(2)}) copy-start(f32[9,64,128]{2,1,0:T(8,128)} %diag_ref.5) | copy-start | bytes 884740
  3.3 18.6 %copy-start.3 = (f32[3,2048]{1,0:T(4,128)S(1)}, f32[3,2048]{1,0:T(4,128)}, u32[]{:S(2)}) copy-start(f32[3,2048]{1,0:T(4,128)} %param_ref.1) | copy-start | bytes 73732
  3.3 18.6 %copy-start.4 = (s32[2048]{0:T(1024)S(1)}, s32[2048]{0:T(1024)}, u32[]{:S(2)}) copy-start(s32[2048]{0:T(1024)} %param.17) | copy-start | bytes 24580
  3.3 18.6 %copy-start.5 = (s32[16]{0:T(128)S(1)}, s32[16]{0:T(128)}, u32[]{:S(2)}) copy-start(s32[16]{0:T(128)} %param.19) | copy-start | bytes 196
  3.4 11.6 %all-to-all-start = ((f32[8,48,128]{2,1,0:T(8,128)}), f32[8,48,128]{2,1,0:T(8,128)S(1)}, u32[]{:S(2)}, u32[]{:S(2)}) async-start(f32[8,48,128]{2,1,0:T(8,128)} %get-tuple-element.17), calls=%async_computation | async-start | bytes 393216 | tf_op jit(solution)/shard_map/all_to_all | solution.py:771
  8.7 13.3 %collective-permute-start.2 = (f32[40,128]{1,0:T(8,128)S(1)}, f32[40,128]{1,0:T(8,128)S(1)}, u32[]{:S(2)}, u32[]{:S(2)}) collective-permute-start(f32[40,128]{1,0:T(8,128)S(1)} %get-tuple-element.24), channel_id=1, source_target_pairs={{0,4},{4,8},{8,12},{12,16},{16,20},{20,24},{24,28},{1,5},{5,9},{9,... | collective-permute-start | bytes 61448 | tf_op jit(solution)/shard_map/ppermute | solution.py:772
  16.8 6.6 %collective-permute-start = (f32[16,128]{1,0:T(8,128)S(1)}, f32[16,128]{1,0:T(8,128)S(1)}, u32[]{:S(2)}, u32[]{:S(2)}) collective-permute-start(f32[16,128]{1,0:T(8,128)S(1)} %get-tuple-element.20.inner_ref), channel_id=1, source_target_pairs={{1,2},{2,1},{5,6},{6,5},{9,10},{10,9},{13,14},{14,13},{17,18},{18,... | collective-permute-start | bytes 24584 | tf_op jit(solution)/shard_map/ppermute | solution.py:802
  17.5 6.1 %collective-permute-start.1 = (f32[16,128]{1,0:T(8,128)S(1)}, f32[16,128]{1,0:T(8,128)S(1)}, u32[]{:S(2)}, u32[]{:S(2)}) collective-permute-start(f32[16,128]{1,0:T(8,128)S(1)} %get-tuple-element.21.outer_ref), channel_id=1, source_target_pairs={{0,1},{2,3},{1,0},{3,2},{4,5},{6,7},{5,4},{7,6},{8,9},{10,11},{9,8... | collective-permute-start | bytes 24584 | tf_op jit(solution)/shard_map/ppermute | solution.py:802

commit v3 on v0

--- a/solution.py
+++ b/solution.py
@@ -69,29 +69,30 @@
 
 
 def pack_kernel(
-    count_ref, values_in, owner_in, node_in, diag_in, edge_in, mask_in, rows_out, strip_ref,
-    values_ref, owner_ref, node_ref, diag_low, diag_high, edge_low, edge_high,
+    count_ref, values_in, owner_in, node_in, diag_in, edge_in, mask_in, rows_out,
+    values_ref, owner_ref, node_ref, diag_low, diag_high, edge_low, edge_high, side_high,
     mask_low, mask_high, rows_ref, arrived, left,
 ):
     targets = rows_ref.shape[0]
     groups = owner_ref.shape[0]
     cells_x = diag_in.shape[1]
     top = pl.ds(cells_x - 8, 8)
+    pieces = [
+        (owner_in, owner_ref),
+        (node_in, node_ref),
+        (values_in, values_ref),
+        (edge_in.at[pl.ds(2, 2), :, top], side_high),
+        (edge_in.at[0, :, top], edge_high),
+        (edge_in.at[1, :, 0:8], edge_low),
+        (mask_in.at[:, top], mask_high),
+        (mask_in.at[1, 0:8], mask_low),
+    ]
+    for k in range(3):
+        pieces.append((diag_in.at[4 * k, top], diag_high.at[k]))
+        pieces.append((diag_in.at[4 * k, 0:8], diag_low.at[k]))
     copies = [
         pltpu.make_async_copy(source, target, arrived.at[k])
-        for k, (source, target) in enumerate(
-            (
-                (owner_in, owner_ref),
-                (node_in, node_ref),
-                (values_in, values_ref),
-                (diag_in.at[:, 0:8], diag_low),
-                (diag_in.at[:, top], diag_high),
-                (mask_in.at[1, 0:8], mask_low),
-                (mask_in.at[:, top], mask_high),
-                (edge_in.at[1, :, 0:8], edge_low),
-                (edge_in.at[:, :, top], edge_high),
-            )
-        )
+        for k, (source, target) in enumerate(pieces)
     ]
     for copy in copies:
         copy.start()
@@ -132,12 +133,11 @@
     for copy in copies[3:]:
         copy.wait()
 
-    def block(edge, mask, direction, at):
-        present = mask[direction, at : at + 1, :].astype(F32)
-        return [edge[direction, k, at : at + 1, :] * present for k in range(9)]
-
-    up_y, low_y = block(edge_high, mask_high, 2, 7), block(edge_high, mask_high, 3, 7)
     here = lax.axis_index("gx")
+
+    def block(edge, mask):
+        present = mask.astype(F32)
+        return [edge(k) * present for k in range(9)]
 
     @pl.when(here < targets - 1)
     def _():
@@ -145,12 +145,14 @@
             rows_ref[here + 1, base + slot : base + slot + 1, :] = value
 
         for k in range(3):
-            put(k, diag_high[4 * k, 7:8, :])
-        for k, value in enumerate(block(edge_high, mask_high, 0, 7)):
-            put(3 + k, value)
+            put(k, diag_high[k, 7:8, :])
+        toward = block(lambda k: edge_high[k, 7:8, :], mask_high[0, 7:8, :])
+        up_y = block(lambda k: side_high[0, k, 7:8, :], mask_high[2, 7:8, :])
+        low_y = block(lambda k: side_high[1, k, 7:8, :], mask_high[3, 7:8, :])
         corners = jnp.zeros((1, LANES), F32)
         lane = iota((1, LANES), 1)
         for k in range(9):
+            put(3 + k, toward[k])
             corners = jnp.where(lane == k, up_y[k][:, LANES - 1 :], corners)
             corners = jnp.where(lane == 9 + k, low_y[k][:, :1], corners)
         put(12, corners)
@@ -161,18 +163,11 @@
             rows_ref[here - 1, base + slot : base + slot + 1, :] = value
 
         for k in range(3):
-            put(k, diag_low[4 * k, 0:1, :])
-        present = mask_low[0:1, :].astype(F32)
-        for k in range(9):
-            put(3 + k, edge_low[k, 0:1, :] * present)
+            put(k, diag_low[k, 0:1, :])
+        for k, value in enumerate(block(lambda k: edge_low[k, 0:1, :], mask_low[0:1, :])):
+            put(3 + k, value)
 
     leaving[1].start()
-    later = [diag_high[k, 7:8, :] for k in range(9) if k % 4]
-    later += up_y + low_y + block(edge_high, mask_high, 0, 6)
-    later += [diag_high[4 * k, 6:7, :] for k in range(3)]
-    for k, value in enumerate(later):
-        strip_ref[k : k + 1, :] = value
-    strip_ref[len(later) :, :] = jnp.zeros((STRIP - len(later), LANES), F32)
     for copy in leaving:
         copy.wait()
 
@@ -189,8 +184,17 @@
 UP_X, LOW_X, INWARD, OUTWARD, WITHIN, INVERSE = 0, 3, 6, 9, 12, 15
 
 
-def edge_kernel(diag_ref, edge_ref, mask_ref, inverse_ref, columns_ref):
+def edge_kernel(diag_ref, edge_ref, mask_ref, inverse_ref, columns_ref, strip_ref):
     cells_x = diag_ref.shape[1]
+    last = cells_x - 1
+    strip = [diag_ref[k, last:, :] for k in range(9) if k % 4]
+    for direction, at in ((2, last), (3, last), (0, last - 1)):
+        present = mask_ref[direction, at : at + 1, :].astype(F32)
+        strip += [edge_ref[direction, k, at : at + 1, :] * present for k in range(9)]
+    strip += [diag_ref[4 * k, last - 1 : last, :] for k in range(3)]
+    for k, value in enumerate(strip):
+        strip_ref[k : k + 1, :] = value
+    strip_ref[len(strip) :, :] = jnp.zeros((STRIP - len(strip), LANES), F32)
     at = iota((cells_x, LANES), 1)
     sides = [jnp.zeros((cells_x, LANES), F32) for _ in range(2)]
 
@@ -739,25 +743,24 @@
         return pltpu.with_memory_space_constraint(array, pltpu.HBM)
 
     i32 = jnp.int32
-    rows, strip = pl.pallas_call(
+    rows = pl.pallas_call(
         pack_kernel,
         in_specs=[SMEM] + [HBM] * 6,
-        out_specs=[HBM, VMEM],
-        out_shape=[
-            pltpu.HBM((width_gx, cells, LANES), F32), pltpu.VMEM((STRIP, LANES), F32)
-        ],
+        out_specs=HBM,
+        out_shape=pltpu.HBM((width_gx, cells, LANES), F32),
         scratch_shapes=[
             pltpu.VMEM(src_values.shape, F32),
             pltpu.VMEM((groups, LANES), i32),
             pltpu.VMEM((groups, LANES), i32),
+            pltpu.VMEM((3, 8, cells_y), F32),
+            pltpu.VMEM((3, 8, cells_y), F32),
             pltpu.VMEM((9, 8, cells_y), F32),
             pltpu.VMEM((9, 8, cells_y), F32),
-            pltpu.VMEM((9, 8, cells_y), F32),
-            pltpu.VMEM((4, 9, 8, cells_y), F32),
+            pltpu.VMEM((2, 9, 8, cells_y), F32),
             pltpu.VMEM((8, cells_y), i32),
             pltpu.VMEM((4, 8, cells_y), i32),
             pltpu.VMEM((width_gx, cells, LANES), F32),
-            pltpu.SemaphoreType.DMA((9,)),
+            pltpu.SemaphoreType.DMA((14,)),
             pltpu.SemaphoreType.DMA((2,)),
         ],
         compiler_params=PARAMS,
@@ -768,20 +771,20 @@
         kept(diag_blocks), kept(edge_blocks), kept(edge_mask),
     )
     rows = lax.all_to_all(rows, "gx", split_axis=0, concat_axis=0, tiled=True)
-    strip = lax.ppermute(strip, "gx", [(i, i + 1) for i in range(width_gx - 1)])
 
     nodes = (3, cells_x, cells_y)
-    inverse, columns = pl.pallas_call(
+    inverse, columns, strip = pl.pallas_call(
         edge_kernel,
         in_specs=[VMEM] * 3,
-        out_specs=[VMEM] * 2,
-        out_shape=[whole(nodes), whole((LANES, LANES))],
+        out_specs=[VMEM] * 3,
+        out_shape=[whole(nodes), whole((LANES, LANES)), whole((STRIP, LANES))],
         compiler_params=PARAMS,
         cost_estimate=pl.CostEstimate(
             flops=10**8, bytes_accessed=4 * 10**6, transcendentals=0
         ),
         name="edge_columns",
     )(diag_blocks, edge_blocks, edge_mask)
+    strip = lax.ppermute(strip, "gx", [(i, i + 1) for i in range(width_gx - 1)])
 
     size = -(-3 * (cells_x + 2 * PAD) // 16) * 16
     field, halo, inner, outer = pl.pallas_call(

time: 35.3 us -> 35.2 us (level)
  no operation moved by 1% of the time
where the time goes in v3:
time: 35.2 us; the launch traced here: 34.9 us
  starting transfers between devices  12.8 us (36%)
  blocking collectives  9.7 us (28%)
  Pallas kernels  7.92 us (22%)
  waiting for transfers between devices  2.85 us (8%)
  between operations  1.52 us (4%)
    all_to_all x1, blocking collectives, per_device(): lax.all_to_all(partial, ('gx', 'gy'), split_axis=0, concat_axis=0, tiled=...  9.7 us
    all_to_all x1, starting transfers between devices, per_device(): rows = lax.all_to_all(rows, 'gx', split_axis=0, concat_axis=0, tiled=True)  5.32 us
    ppermute x2, starting transfers between devices, swapped(): return lax.ppermute(columns, 'gy', pairs)  5.11 us
    all_to_all x1, waiting for transfers between devices, per_device(): rows = lax.all_to_all(rows, 'gx', split_axis=0, concat_axis=0, tiled=True)  2.7 us
    ppermute x1, starting transfers between devices, per_device(): strip = lax.ppermute(strip, 'gx', [(i, i + 1) for i in range(width_gx - 1)])  2.4 us
    pallas_call x1, Pallas kernels, per_device(): pl.pallas_call(field_kernel, in_specs=[VMEM] * 3, out_specs=[VMEM] * 4, o...  1.91 us
    pallas_call x1, Pallas kernels, per_device(): pl.pallas_call(pack_kernel, in_specs=[SMEM] + [HBM] * 6, out_specs=HBM, o...  1.82 us
    pallas_call x1, Pallas kernels, per_device(): pl.pallas_call(functools.partial(box_kernel, tile_points=points // tiles)...  1.44 us
  transfers between devices with their start and end apart: 4, of which 2 were waited for; matrix products, arithmetic and copies ran while one was open for 0% of the time, Pallas kernels for 13%

profile of v3, /device:TPU:0, one launch (start us, length us, event | category | flops | bytes accessed | tf_op | source)
XLA Modules:
  0.0 34.9 jit_solution(10358511706463430652)
XLA Ops:
  0.6 0.0 copy-start.2
  0.6 0.0 copy-start
  0.7 0.0 copy-start.1
  1.4 1.8 %pack_rows_and_edges.1 = f32[8,48,128]{2,1,0:T(8,128)} custom-call(s32[1]{0:T(128)S(6)} %copy.12.count_ref, f32[3,1024]{1,0:T(4,128)} %values_in.1, s32[8,128]{1,0:T(8,128)} %bitcast.6, s32[8,128]{1,0:T(8,128)} %bitcast.7, f32[9,64,128]{2,1,0:T(8,128)} %diag_ref.5, f32[4,9,64,128]{3,2,1,0:T(8,128)} %edge_ref.5, s32[4,64,128]{2,1,0:T(8,128)} %mask_ref.5), custom_call_target="tpu_custom_call" | custom-call | tf_op jit(solution)/shard_map/pack_rows_and_edges/pallas_call | solution.py:746
  3.3 0.0 copy-start.3
  3.3 0.0 copy-start.4
  3.3 0.0 copy-start.5
  3.3 5.3 %all-to-all-start = ((f32[8,48,128]{2,1,0:T(8,128)}), f32[8,48,128]{2,1,0:T(8,128)S(1)}, u32[]{:S(2)}, u32[]{:S(2)}) async-start(f32[8,48,128]{2,1,0:T(8,128)} %pack_rows_and_edges.1), calls=%async_computation | async-start | bytes 393216 | tf_op jit(solution)/shard_map/all_to_all | solution.py:773
  8.6 0.0 copy-done.2
  8.6 0.0 copy-done
  8.6 1.1 %edge_columns.1 = (f32[3,64,128]{2,1,0:T(8,128)S(1)}, f32[128,128]{1,0:T(8,128)S(1)}, f32[40,128]{1,0:T(8,128)S(1)}) custom-call(f32[9,64,128]{2,1,0:T(8,128)S(1)} %copy-done.1, f32[4,9,64,128]{3,2,1,0:T(8,128)S(1)} %copy-done, s32[4,64,128]{2,1,0:T(8,128)S(1)} %copy-done.2), custom_call_target="tpu_custom_call" | custom-call | flops 100000000 | bytes 4000000 | tf_op jit(solution)/shard_map/edge_columns/pallas_call | solution.py:776
  9.7 2.4 %collective-permute-start.2 = (f32[40,128]{1,0:T(8,128)S(1)}, f32[40,128]{1,0:T(8,128)S(1)}, u32[]{:S(2)}, u32[]{:S(2)}) collective-permute-start(f32[40,128]{1,0:T(8,128)S(1)} %get-tuple-element.22), channel_id=1, source_target_pairs={{0,4},{4,8},{8,12},{12,16},{16,20},{20,24},{24,28},{1,5},{5,9},{9,... | collective-permute-start | bytes 61448 | tf_op jit(solution)/shard_map/ppermute | solution.py:787
  12.1 2.7 %all-to-all-done.rows_ref = f32[8,48,128]{2,1,0:T(8,128)S(1)} async-done(((f32[8,48,128]{2,1,0:T(8,128)}), f32[8,48,128]{2,1,0:T(8,128)S(1)}, u32[]{:S(2)}, u32[]{:S(2)}) %all-to-all-start) | async-done | bytes 196640 | tf_op jit(solution)/shard_map/all_to_all | solution.py:773
  14.8 1.9 %load_and_first_product.1 = (f32[3,64,128]{2,1,0:T(8,128)S(1)}, f32[24,128]{1,0:T(8,128)S(1)}, f32[16,128]{1,0:T(8,128)S(1)}, f32[16,128]{1,0:T(8,128)S(1)}) custom-call(f32[8,48,128]{2,1,0:T(8,128)S(1)} %all-to-all-done.rows_ref, f32[3,64,128]{2,1,0:T(8,128)S(1)} %get-tuple-element.16.inverse_ref, f32[128,128]{1,0:T(8,128)S(1)} %get-tuple-element.17.columns_ref), custom_call_target="tpu_custom_call" | custom-call | tf_op jit(solution)/shard_map/load_and_first_product/pallas_call | solution.py:790
  16.8 0.7 %collective-permute-start = (f32[16,128]{1,0:T(8,128)S(1)}, f32[16,128]{1,0:T(8,128)S(1)}, u32[]{:S(2)}, u32[]{:S(2)}) collective-permute-start(f32[16,128]{1,0:T(8,128)S(1)} %get-tuple-element.18.inner_ref), channel_id=1, source_target_pairs={{1,2},{2,1},{5,6},{6,5},{9,10},{10,9},{13,14},{14,13},{17,18},{18,... | collective-permute-start | bytes 24584 | tf_op jit(solution)/shard_map/ppermute | solution.py:804
  17.4 4.5 %collective-permute-start.1 = (f32[16,128]{1,0:T(8,128)S(1)}, f32[16,128]{1,0:T(8,128)S(1)}, u32[]{:S(2)}, u32[]{:S(2)}) collective-permute-start(f32[16,128]{1,0:T(8,128)S(1)} %get-tuple-element.19.outer_ref), channel_id=1, source_target_pairs={{0,1},{2,3},{1,0},{3,2},{4,5},{6,7},{5,4},{7,6},{8,9},{10,11},{9,8... | collective-permute-start | bytes 24584 | tf_op jit(solution)/shard_map/ppermute | solution.py:804
  21.9 0.0 collective-permute-done.2.strip_ref
  21.9 0.0 copy-done.4
  21.9 1.4 %box_parts.1 = (f32[3,64,128]{2,1,0:T(8,128)S(1)}, f32[128,128]{1,0:T(8,128)S(1)}, bf16[128,2048]{1,0:T(8,128)(2,1)S(1)}, f32[8,128]{1,0:T(8,128)S(1)}, bf16[128,128]{1,0:T(8,128)(2,1)S(1)}) custom-call(s32[1,16]{1,0:T(1,128)S(1)} %bitcast.5, f32[3,64,128]{2,1,0:T(8,128)S(1)} %get-tuple-element.20.field_ref, s32[16,128]{1,0:T(8,128)S(1)} %bitcast.4, ...), custom_call_target="tpu_custom_call" | custom-call | flops 1000000000 | bytes 4000000 | tf_op jit(solution)/shard_map/box_parts/pallas_call | solution.py:808
  23.3 0.0 collective-permute-done.from_inner_ref
  23.4 0.1 collective-permute-done.1.from_outer_ref
  23.5 0.6 %sums_and_halo_parts.1 = (f32[3,64,128]{2,1,0:T(8,128)S(1)}, f32[32,4,128]{2,1,0:T(4,128)S(1)}) custom-call(f32[16,128]{1,0:T(8,128)S(1)} %collective-permute-done.from_inner_ref, f32[16,128]{1,0:T(8,128)S(1)} %collective-permute-done.1.from_outer_ref, f32[16,128]{1,0:T(8,128)S(1)} %get-tuple-element.18.inner_ref, ...), custom_call_target="tpu_custom_call" | custom-call | tf_op jit(solution)/shard_map/sums_and_halo_parts/pallas_call | solution.py:833
  24.1 9.7 %all_to_all.10.got_ref = f32[32,4,128]{2,1,0:T(4,128)S(1)} all-to-all(f32[32,4,128]{2,1,0:T(4,128)S(1)} %get-tuple-element.28), channel_id=1, replica_groups=mesh['gx'=8,'gy'=4] {'gx','gy'}, dimensions={0} | all-to-all | bytes 131072 | tf_op jit(solution)/shard_map/all_to_all | solution.py:844
  33.8 1.0 %steps_and_outputs.1 = (f32[3,64,128]{2,1,0:T(8,128)}, f32[1,192]{1,0:T(1,128)}) custom-call(f32[32,4,128]{2,1,0:T(4,128)S(1)} %all_to_all.10.got_ref, f32[3,64,128]{2,1,0:T(8,128)S(1)} %get-tuple-element.20.field_ref, f32[3,64,128]{2,1,0:T(8,128)S(1)} %get-tuple-element.29.quotient_ref), custom_call_target="tpu_custom_call" | custom-call | tf_op jit(solution)/shard_map/steps_and_outputs/pallas_call | solution.py:845
  (3 shorter events, 0.0 us)
Async XLA Ops:
  0.6 8.0 %copy-start.2 = (s32[4,64,128]{2,1,0:T(8,128)S(1)}, s32[4,64,128]{2,1,0:T(8,128)}, u32[]{:S(2)}) copy-start(s32[4,64,128]{2,1,0:T(8,128)} %mask_ref.5) | copy-start | bytes 393220
  0.6 8.0 %copy-start = (f32[4,9,64,128]{3,2,1,0:T(8,128)S(1)}, f32[4,9,64,128]{3,2,1,0:T(8,128)}, u32[]{:S(2)}) copy-start(f32[4,9,64,128]{3,2,1,0:T(8,128)} %edge_ref.5) | copy-start | bytes 3538948
  0.7 8.0 %copy-start.1 = (f32[9,64,128]{2,1,0:T(8,128)S(1)}, f32[9,64,128]{2,1,0:T(8,128)}, u32[]{:S(2)}) copy-start(f32[9,64,128]{2,1,0:T(8,128)} %diag_ref.5) | copy-start | bytes 884740
  3.3 18.6 %copy-start.3 = (f32[3,2048]{1,0:T(4,128)S(1)}, f32[3,2048]{1,0:T(4,128)}, u32[]{:S(2)}) copy-start(f32[3,2048]{1,0:T(4,128)} %param_ref.1) | copy-start | bytes 73732
  3.3 18.6 %copy-start.4 = (s32[2048]{0:T(1024)S(1)}, s32[2048]{0:T(1024)}, u32[]{:S(2)}) copy-start(s32[2048]{0:T(1024)} %param.17) | copy-start | bytes 24580
  3.3 18.6 %copy-start.5 = (s32[16]{0:T(128)S(1)}, s32[16]{0:T(128)}, u32[]{:S(2)}) copy-start(s32[16]{0:T(128)} %param.19) | copy-start | bytes 196
  3.3 11.6 %all-to-all-start = ((f32[8,48,128]{2,1,0:T(8,128)}), f32[8,48,128]{2,1,0:T(8,128)S(1)}, u32[]{:S(2)}, u32[]{:S(2)}) async-start(f32[8,48,128]{2,1,0:T(8,128)} %pack_rows_and_edges.1), calls=%async_computation | async-start | bytes 393216 | tf_op jit(solution)/shard_map/all_to_all | solution.py:773
  9.7 12.1 %collective-permute-start.2 = (f32[40,128]{1,0:T(8,128)S(1)}, f32[40,128]{1,0:T(8,128)S(1)}, u32[]{:S(2)}, u32[]{:S(2)}) collective-permute-start(f32[40,128]{1,0:T(8,128)S(1)} %get-tuple-element.22), channel_id=1, source_target_pairs={{0,4},{4,8},{8,12},{12,16},{16,20},{20,24},{24,28},{1,5},{5,9},{9,... | collective-permute-start | bytes 61448 | tf_op jit(solution)/shard_map/ppermute | solution.py:787
  16.8 6.6 %collective-permute-start = (f32[16,128]{1,0:T(8,128)S(1)}, f32[16,128]{1,0:T(8,128)S(1)}, u32[]{:S(2)}, u32[]{:S(2)}) collective-permute-start(f32[16,128]{1,0:T(8,128)S(1)} %get-tuple-element.18.inner_ref), channel_id=1, source_target_pairs={{1,2},{2,1},{5,6},{6,5},{9,10},{10,9},{13,14},{14,13},{17,18},{18,... | collective-permute-start | bytes 24584 | tf_op jit(solution)/shard_map/ppermute | solution.py:804
  17.4 6.1 %collective-permute-start.1 = (f32[16,128]{1,0:T(8,128)S(1)}, f32[16,128]{1,0:T(8,128)S(1)}, u32[]{:S(2)}, u32[]{:S(2)}) collective-permute-start(f32[16,128]{1,0:T(8,128)S(1)} %get-tuple-element.19.outer_ref), channel_id=1, source_target_pairs={{0,1},{2,3},{1,0},{3,2},{4,5},{6,7},{5,4},{7,6},{8,9},{10,11},{9,8... | collective-permute-start | bytes 24584 | tf_op jit(solution)/shard_map/ppermute | solution.py:804

commit v4 on v3

--- a/solution.py
+++ b/solution.py
@@ -1,5 +1,4 @@
 import functools
-import math
 
 import jax
 import jax.numpy as jnp
@@ -69,7 +68,7 @@
 
 
 def pack_kernel(
-    count_ref, values_in, owner_in, node_in, diag_in, edge_in, mask_in, rows_out,
+    count_ref, values_in, owner_in, node_in, diag_in, edge_in, mask_in, rows_out, own_ref,
     values_ref, owner_ref, node_ref, diag_low, diag_high, edge_low, edge_high, side_high,
     mask_low, mask_high, rows_ref, arrived, left,
 ):
@@ -168,6 +167,7 @@
             put(3 + k, value)
 
     leaving[1].start()
+    own_ref[...] = rows_ref[here, : 4 * groups, :]
     for copy in leaving:
         copy.wait()
 
@@ -222,29 +222,18 @@
     columns_ref[...] = jnp.concatenate(sides, axis=0).T
 
 
-def field_kernel(
-    rows_ref, inverse_ref, columns_ref,
-    field_ref, halo_ref, inner_ref, outer_ref, load_ref,
-):
-    senders = rows_ref.shape[0]
-    groups = (rows_ref.shape[1] - NEAR) // 4
-    cells_x = field_ref.shape[1]
-    half = (cells_x + 2 * PAD) // 2
-    own = cells_x // 2
-
-    load_ref[...] = jnp.zeros_like(load_ref)
-    here = lax.axis_index("gx")
-
-    size = load_ref.shape[0]
+def load_product(blocks, half):
+    groups = blocks[0].shape[0] // 4
+    size = -(-6 * half // 16) * 16
     line = iota((size, LANES), 0)
     block = sum(jnp.where(line >= half * k, 1, 0) for k in range(1, 6))
     at_row = jnp.where(line < 6 * half, line - half * block, -5).astype(F32).astype(BF16)
     at_column = float_iota((2 * LANES, LANES), 0).astype(BF16)
     in_tile = float_iota((16, LANES), 0).astype(BF16)
     zero, one = jnp.zeros((), BF16), jnp.ones((), BF16)
-
-    def operands(sender):
-        index = rows_ref[sender, 3 * groups : 4 * groups, :]
+    lefts, rights = [], []
+    for rows in blocks:
+        index = rows[3 * groups :]
         split = float(half * LANES)
         index, shift = (
             jnp.where(index >= split, index - split, index),
@@ -252,14 +241,11 @@
         )
         place = jnp.floor(index * (1.0 / LANES))
         column = index - place * float(LANES) + shift
-        parts = [
-            two_parts(rows_ref[sender, c * groups : (c + 1) * groups, :]) for c in range(3)
-        ]
-        lefts, rights = [], []
+        parts = [two_parts(rows[c * groups : (c + 1) * groups]) for c in range(3)]
         for group in range(groups):
-            line = slice(group, group + 1)
+            here = slice(group, group + 1)
             values = [
-                stretched(parts[c][which][line], 16) for which in range(2) for c in range(3)
+                stretched(parts[c][which][here], 16) for which in range(2) for c in range(3)
             ]
             tiles = []
             for first in range(0, size, 16):
@@ -271,31 +257,48 @@
                         in_tile < float(half * high - first), values[low], values[high]
                     )
                 )
-            match = at_row == stretched(place[line], size)
+            match = at_row == stretched(place[here], size)
             lefts.append(jnp.where(match, jnp.concatenate(tiles, axis=0), zero))
             rights.append(
-                jnp.where(at_column == stretched(column[line], 2 * LANES), one, zero)
+                jnp.where(at_column == stretched(column[here], 2 * LANES), one, zero)
             )
-        return lefts, rights
-
-    together = math.gcd(senders, 4)
+    return lax.dot_general(
+        jnp.concatenate(lefts, axis=1),
+        jnp.concatenate(rights, axis=1),
+        (((1,), (1,)), ((), ())),
+        preferred_element_type=F32,
+    )
+
+
+def own_kernel(rows_ref, load_ref, *, half):
+    load_ref[...] = load_product([rows_ref[...]], half)
+
+
+def field_kernel(
+    rows_ref, own_ref, inverse_ref, columns_ref,
+    field_ref, halo_ref, inner_ref, outer_ref, load_ref,
+):
+    senders = rows_ref.shape[0]
+    groups = (rows_ref.shape[1] - NEAR) // 4
+    cells_x = field_ref.shape[1]
+    half = (cells_x + 2 * PAD) // 2
+    own = cells_x // 2
+
+    load_ref[...] = own_ref[...]
+    here = lax.axis_index("gx")
+    others = senders - 1
+    together = others if others <= 8 else 1
 
     def add_rows(step, carry):
-        lefts, rights = [], []
+        blocks = []
         for k in range(together):
-            left, right = operands(step * together + k)
-            lefts += left
-            rights += right
-        load_ref[...] += lax.dot_general(
-            jnp.concatenate(lefts, axis=1),
-            jnp.concatenate(rights, axis=1),
-            (((1,), (1,)), ((), ())),
-            preferred_element_type=F32,
-        )
+            sender = step * together + k
+            sender = jnp.where(sender >= here, sender + 1, sender)
+            blocks.append(rows_ref[sender, : 4 * groups, :])
+        load_ref[...] += load_product(blocks, half)
         return carry
 
-    steps = senders // together
-    lax.fori_loop(0, steps, add_rows, 0, unroll=min(steps, 2))
+    lax.fori_loop(0, others // together, add_rows, 0)
 
     def load_rows(comp, first, last, second_half):
         lanes = slice(LANES, 2 * LANES) if second_half else slice(0, LANES)
@@ -743,11 +746,14 @@
         return pltpu.with_memory_space_constraint(array, pltpu.HBM)
 
     i32 = jnp.int32
-    rows = pl.pallas_call(
+    rows, own = pl.pallas_call(
         pack_kernel,
         in_specs=[SMEM] + [HBM] * 6,
-        out_specs=HBM,
-        out_shape=pltpu.HBM((width_gx, cells, LANES), F32),
+        out_specs=[HBM, VMEM],
+        out_shape=[
+            pltpu.HBM((width_gx, cells, LANES), F32),
+            pltpu.VMEM((4 * groups, LANES), F32),
+        ],
         scratch_shapes=[
             pltpu.VMEM(src_values.shape, F32),
             pltpu.VMEM((groups, LANES), i32),
@@ -786,10 +792,22 @@
     )(diag_blocks, edge_blocks, edge_mask)
     strip = lax.ppermute(strip, "gx", [(i, i + 1) for i in range(width_gx - 1)])
 
-    size = -(-3 * (cells_x + 2 * PAD) // 16) * 16
+    half = (cells_x + 2 * PAD) // 2
+    size = -(-6 * half // 16) * 16
+    own_load = pl.pallas_call(
+        functools.partial(own_kernel, half=half),
+        in_specs=[VMEM],
+        out_specs=VMEM,
+        out_shape=whole((size, 2 * LANES)),
+        compiler_params=PARAMS,
+        cost_estimate=pl.CostEstimate(
+            flops=10**8, bytes_accessed=10**6, transcendentals=0
+        ),
+        name="own_load",
+    )(own)
     field, halo, inner, outer = pl.pallas_call(
         field_kernel,
-        in_specs=[VMEM] * 3,
+        in_specs=[VMEM] * 4,
         out_specs=[VMEM] * 4,
         out_shape=[
             whole(nodes), whole((24, cells_y)), whole((16, LANES)), whole((16, LANES)),
@@ -797,7 +815,7 @@
         scratch_shapes=[pltpu.VMEM((size, 2 * LANES), F32)],
         compiler_params=PARAMS,
         name="load_and_first_product",
-    )(rows, inverse, columns)
+    )(rows, own_load, inverse, columns)
     def swapped(columns, first):
         low = range(first, width_gy - 1, 2)
         pairs = [(i, i + 1) for i in low] + [(i + 1, i) for i in low]

time: 35.2 us -> 34.8 us (0.989)
  waiting for transfers between devices: 2.85 us -> 2.45 us
    all_to_all x1, waiting for transfers between devices: 2.7 us -> 2.31 us  [per_device(): rows = lax.all_to_all(rows, 'gx', split_axis=0, concat_axis=0, tiled=True)]
    pallas_call x2 -> x3, Pallas kernels: 3.73 us -> 3.93 us  [the longest x1 1.82 us: per_device(): pl.pallas_call(pack_kernel, in_specs=[SMEM] + [HBM] * 6, out_specs=[HBM,...]
  transfers between devices with their start and end apart: 4 -> 4, of which waited for: 2 -> 2; matrix products, arithmetic and copies ran while one was open for 0% -> 0% of each run, Pallas kernels for 13% -> 14%
where the time goes in v4:
time: 34.8 us; the launch traced here: 34.5 us
  starting transfers between devices  12.7 us (36%)
  blocking collectives  9.69 us (28%)
  Pallas kernels  8.13 us (23%)
  waiting for transfers between devices  2.45 us (7%)
  between operations  1.53 us (4%)
    all_to_all x1, blocking collectives, per_device(): lax.all_to_all(partial, ('gx', 'gy'), split_axis=0, concat_axis=0, tiled=...  9.69 us
    all_to_all x1, starting transfers between devices, per_device(): rows = lax.all_to_all(rows, 'gx', split_axis=0, concat_axis=0, tiled=True)  5.19 us
    ppermute x2, starting transfers between devices, swapped(): return lax.ppermute(columns, 'gy', pairs)  5.12 us
    ppermute x1, starting transfers between devices, per_device(): strip = lax.ppermute(strip, 'gx', [(i, i + 1) for i in range(width_gx - 1)])  2.4 us
    all_to_all x1, waiting for transfers between devices, per_device(): rows = lax.all_to_all(rows, 'gx', split_axis=0, concat_axis=0, tiled=True)  2.31 us
    pallas_call x1, Pallas kernels, per_device(): pl.pallas_call(pack_kernel, in_specs=[SMEM] + [HBM] * 6, out_specs=[HBM,...  1.82 us
    pallas_call x1, Pallas kernels, per_device(): pl.pallas_call(field_kernel, in_specs=[VMEM] * 4, out_specs=[VMEM] * 4, o...  1.76 us
    pallas_call x1, Pallas kernels, per_device(): pl.pallas_call(functools.partial(box_kernel, tile_points=points // tiles)...  1.46 us
  transfers between devices with their start and end apart: 4, of which 2 were waited for; matrix products, arithmetic and copies ran while one was open for 0% of the time, Pallas kernels for 14%

profile of v4, /device:TPU:0, one launch (start us, length us, event | category | flops | bytes accessed | tf_op | source)
XLA Modules:
  0.0 34.5 jit_solution(903223095059695302)
XLA Ops:
  0.6 0.0 copy-start.2
  0.6 0.0 copy-start
  0.7 0.0 copy-start.1
  1.4 1.8 %pack_rows_and_edges.1 = (f32[8,48,128]{2,1,0:T(8,128)}, f32[32,128]{1,0:T(8,128)S(1)}) custom-call(s32[1]{0:T(128)S(6)} %copy.12.count_ref, f32[3,1024]{1,0:T(4,128)} %values_in.1, s32[8,128]{1,0:T(8,128)} %bitcast.6, s32[8,128]{1,0:T(8,128)} %bitcast.7, f32[9,64,128]{2,1,0:T(8,128)} %diag_ref.5, f32[4,9,64,128]{3,2,1,0:T(8,128)} %edge_ref.5, ...), custom_call_target="tpu_custom_call" | custom-call | tf_op jit(solution)/shard_map/pack_rows_and_edges/pallas_call | solution.py:749
  3.3 5.2 %all-to-all-start = ((f32[8,48,128]{2,1,0:T(8,128)}), f32[8,48,128]{2,1,0:T(8,128)S(1)}, u32[]{:S(2)}, u32[]{:S(2)}) async-start(f32[8,48,128]{2,1,0:T(8,128)} %get-tuple-element.18), calls=%async_computation | async-start | bytes 393216 | tf_op jit(solution)/shard_map/all_to_all | solution.py:779
  8.4 0.0 copy-done.2
  8.5 0.0 copy-start.3
  8.5 0.0 copy-start.4
  8.5 0.0 copy-start.5
  8.5 1.1 %edge_columns.1 = (f32[3,64,128]{2,1,0:T(8,128)S(1)}, f32[128,128]{1,0:T(8,128)S(1)}, f32[40,128]{1,0:T(8,128)S(1)}) custom-call(f32[9,64,128]{2,1,0:T(8,128)S(1)} %copy-done.1, f32[4,9,64,128]{3,2,1,0:T(8,128)S(1)} %copy-done, s32[4,64,128]{2,1,0:T(8,128)S(1)} %copy-done.2), custom_call_target="tpu_custom_call" | custom-call | flops 100000000 | bytes 4000000 | tf_op jit(solution)/shard_map/edge_columns/pallas_call | solution.py:782
  9.6 2.4 %collective-permute-start.2 = (f32[40,128]{1,0:T(8,128)S(1)}, f32[40,128]{1,0:T(8,128)S(1)}, u32[]{:S(2)}, u32[]{:S(2)}) collective-permute-start(f32[40,128]{1,0:T(8,128)S(1)} %get-tuple-element.26), channel_id=1, source_target_pairs={{0,4},{4,8},{8,12},{12,16},{16,20},{20,24},{24,28},{1,5},{5,9},{9,... | collective-permute-start | bytes 61448 | tf_op jit(solution)/shard_map/ppermute | solution.py:793
  12.0 0.3 %own_load.1.own_ref = f32[208,256]{1,0:T(8,128)S(1)} custom-call(f32[32,128]{1,0:T(8,128)S(1)} %get-tuple-element.19.rows_ref), custom_call_target="tpu_custom_call" | custom-call | flops 100000000 | bytes 1000000 | tf_op jit(solution)/shard_map/own_load/pallas_call | solution.py:797
  12.4 2.3 %all-to-all-done.rows_ref = f32[8,48,128]{2,1,0:T(8,128)S(1)} async-done(((f32[8,48,128]{2,1,0:T(8,128)}), f32[8,48,128]{2,1,0:T(8,128)S(1)}, u32[]{:S(2)}, u32[]{:S(2)}) %all-to-all-start) | async-done | bytes 196640 | tf_op jit(solution)/shard_map/all_to_all | solution.py:779
  14.7 1.8 %load_and_first_product.1 = (f32[3,64,128]{2,1,0:T(8,128)S(1)}, f32[24,128]{1,0:T(8,128)S(1)}, f32[16,128]{1,0:T(8,128)S(1)}, f32[16,128]{1,0:T(8,128)S(1)}) custom-call(f32[8,48,128]{2,1,0:T(8,128)S(1)} %all-to-all-done.rows_ref, f32[208,256]{1,0:T(8,128)S(1)} %own_load.1.own_ref, f32[3,64,128]{2,1,0:T(8,128)S(1)} %get-tuple-element.20.inverse_ref, ...), custom_call_target="tpu_custom_call" | custom-call | tf_op jit(solution)/shard_map/load_and_first_product/pallas_call | solution.py:808
  16.4 0.7 %collective-permute-start = (f32[16,128]{1,0:T(8,128)S(1)}, f32[16,128]{1,0:T(8,128)S(1)}, u32[]{:S(2)}, u32[]{:S(2)}) collective-permute-start(f32[16,128]{1,0:T(8,128)S(1)} %get-tuple-element.22.inner_ref), channel_id=1, source_target_pairs={{1,2},{2,1},{5,6},{6,5},{9,10},{10,9},{13,14},{14,13},{17,18},{18,... | collective-permute-start | bytes 24584 | tf_op jit(solution)/shard_map/ppermute | solution.py:822
  17.1 4.5 %collective-permute-start.1 = (f32[16,128]{1,0:T(8,128)S(1)}, f32[16,128]{1,0:T(8,128)S(1)}, u32[]{:S(2)}, u32[]{:S(2)}) collective-permute-start(f32[16,128]{1,0:T(8,128)S(1)} %get-tuple-element.23.outer_ref), channel_id=1, source_target_pairs={{0,1},{2,3},{1,0},{3,2},{4,5},{6,7},{5,4},{7,6},{8,9},{10,11},{9,8... | collective-permute-start | bytes 24584 | tf_op jit(solution)/shard_map/ppermute | solution.py:822
  21.6 0.0 collective-permute-done.2.strip_ref
  21.6 0.0 copy-done.4
  21.6 1.5 %box_parts.1 = (f32[3,64,128]{2,1,0:T(8,128)S(1)}, f32[128,128]{1,0:T(8,128)S(1)}, bf16[128,2048]{1,0:T(8,128)(2,1)S(1)}, f32[8,128]{1,0:T(8,128)S(1)}, bf16[128,128]{1,0:T(8,128)(2,1)S(1)}) custom-call(s32[1,16]{1,0:T(1,128)S(1)} %bitcast.5, f32[3,64,128]{2,1,0:T(8,128)S(1)} %get-tuple-element.24.field_ref, s32[16,128]{1,0:T(8,128)S(1)} %bitcast.4, ...), custom_call_target="tpu_custom_call" | custom-call | flops 1000000000 | bytes 4000000 | tf_op jit(solution)/shard_map/box_parts/pallas_call | solution.py:826
  23.1 0.0 collective-permute-done.from_inner_ref
  23.1 0.1 collective-permute-done.1.from_outer_ref
  23.2 0.6 %sums_and_halo_parts.1 = (f32[3,64,128]{2,1,0:T(8,128)S(1)}, f32[32,4,128]{2,1,0:T(4,128)S(1)}) custom-call(f32[16,128]{1,0:T(8,128)S(1)} %collective-permute-done.from_inner_ref, f32[16,128]{1,0:T(8,128)S(1)} %collective-permute-done.1.from_outer_ref, f32[16,128]{1,0:T(8,128)S(1)} %get-tuple-element.22.inner_ref, ...), custom_call_target="tpu_custom_call" | custom-call | tf_op jit(solution)/shard_map/sums_and_halo_parts/pallas_call | solution.py:851
  23.8 9.7 %all_to_all.10.got_ref = f32[32,4,128]{2,1,0:T(4,128)S(1)} all-to-all(f32[32,4,128]{2,1,0:T(4,128)S(1)} %get-tuple-element.32), channel_id=1, replica_groups=mesh['gx'=8,'gy'=4] {'gx','gy'}, dimensions={0} | all-to-all | bytes 131072 | tf_op jit(solution)/shard_map/all_to_all | solution.py:862
  33.5 1.0 %steps_and_outputs.1 = (f32[3,64,128]{2,1,0:T(8,128)}, f32[1,192]{1,0:T(1,128)}) custom-call(f32[32,4,128]{2,1,0:T(4,128)S(1)} %all_to_all.10.got_ref, f32[3,64,128]{2,1,0:T(8,128)S(1)} %get-tuple-element.24.field_ref, f32[3,64,128]{2,1,0:T(8,128)S(1)} %get-tuple-element.33.quotient_ref), custom_call_target="tpu_custom_call" | custom-call | tf_op jit(solution)/shard_map/steps_and_outputs/pallas_call | solution.py:863
  (4 shorter events, 0.0 us)
Async XLA Ops:
  0.6 7.8 %copy-start.2 = (s32[4,64,128]{2,1,0:T(8,128)S(1)}, s32[4,64,128]{2,1,0:T(8,128)}, u32[]{:S(2)}) copy-start(s32[4,64,128]{2,1,0:T(8,128)} %mask_ref.5) | copy-start | bytes 393220
  0.6 7.8 %copy-start = (f32[4,9,64,128]{3,2,1,0:T(8,128)S(1)}, f32[4,9,64,128]{3,2,1,0:T(8,128)}, u32[]{:S(2)}) copy-start(f32[4,9,64,128]{3,2,1,0:T(8,128)} %edge_ref.5) | copy-start | bytes 3538948
  0.7 7.8 %copy-start.1 = (f32[9,64,128]{2,1,0:T(8,128)S(1)}, f32[9,64,128]{2,1,0:T(8,128)}, u32[]{:S(2)}) copy-start(f32[9,64,128]{2,1,0:T(8,128)} %diag_ref.5) | copy-start | bytes 884740
  3.3 11.4 %all-to-all-start = ((f32[8,48,128]{2,1,0:T(8,128)}), f32[8,48,128]{2,1,0:T(8,128)S(1)}, u32[]{:S(2)}, u32[]{:S(2)}) async-start(f32[8,48,128]{2,1,0:T(8,128)} %get-tuple-element.18), calls=%async_computation | async-start | bytes 393216 | tf_op jit(solution)/shard_map/all_to_all | solution.py:779
  8.5 13.1 %copy-start.3 = (f32[3,2048]{1,0:T(4,128)S(1)}, f32[3,2048]{1,0:T(4,128)}, u32[]{:S(2)}) copy-start(f32[3,2048]{1,0:T(4,128)} %param_ref.1) | copy-start | bytes 73732
  8.5 13.1 %copy-start.4 = (s32[2048]{0:T(1024)S(1)}, s32[2048]{0:T(1024)}, u32[]{:S(2)}) copy-start(s32[2048]{0:T(1024)} %param.17) | copy-start | bytes 24580
  8.5 13.1 %copy-start.5 = (s32[16]{0:T(128)S(1)}, s32[16]{0:T(128)}, u32[]{:S(2)}) copy-start(s32[16]{0:T(128)} %param.19) | copy-start | bytes 196
  9.6 12.0 %collective-permute-start.2 = (f32[40,128]{1,0:T(8,128)S(1)}, f32[40,128]{1,0:T(8,128)S(1)}, u32[]{:S(2)}, u32[]{:S(2)}) collective-permute-start(f32[40,128]{1,0:T(8,128)S(1)} %get-tuple-element.26), channel_id=1, source_target_pairs={{0,4},{4,8},{8,12},{12,16},{16,20},{20,24},{24,28},{1,5},{5,9},{9,... | collective-permute-start | bytes 61448 | tf_op jit(solution)/shard_map/ppermute | solution.py:793
  16.4 6.6 %collective-permute-start = (f32[16,128]{1,0:T(8,128)S(1)}, f32[16,128]{1,0:T(8,128)S(1)}, u32[]{:S(2)}, u32[]{:S(2)}) collective-permute-start(f32[16,128]{1,0:T(8,128)S(1)} %get-tuple-element.22.inner_ref), channel_id=1, source_target_pairs={{1,2},{2,1},{5,6},{6,5},{9,10},{10,9},{13,14},{14,13},{17,18},{18,... | collective-permute-start | bytes 24584 | tf_op jit(solution)/shard_map/ppermute | solution.py:822
  17.1 6.1 %collective-permute-start.1 = (f32[16,128]{1,0:T(8,128)S(1)}, f32[16,128]{1,0:T(8,128)S(1)}, u32[]{:S(2)}, u32[]{:S(2)}) collective-permute-start(f32[16,128]{1,0:T(8,128)S(1)} %get-tuple-element.23.outer_ref), channel_id=1, source_target_pairs={{0,1},{2,3},{1,0},{3,2},{4,5},{6,7},{5,4},{7,6},{8,9},{10,11},{9,8... | collective-permute-start | bytes 24584 | tf_op jit(solution)/shard_map/ppermute | solution.py:822

commit v5 on v4

--- a/solution.py
+++ b/solution.py
@@ -339,26 +339,30 @@
     lane_row = iota((1, LANES), 1)
     ends = jnp.zeros((1, LANES), F32)
     for i in range(3):
-        for a in range(3):
-            ends = jnp.where(lane_row == 3 * i + a, before[2][i][:, LANES - 1 :], ends)
-            ends = jnp.where(lane_row == 9 + 3 * i + a, before[2][i][:, :1], ends)
+        for first, end in ((3 * i, LANES - 1), (9 + 3 * i, 0)):
+            mine = (lane_row >= first) & (lane_row < first + 3)
+            ends = jnp.where(mine, before[2][i][:, end : end + 1], ends)
     ends = ends * rows_ref[lower, base + 12 : base + 13, :]
     ends = ends + pltpu.roll(ends, LANES - 3, 1) + pltpu.roll(ends, LANES - 6, 1)
 
-    at = iota((cells_x, LANES), 1)
-    sides = []
-    for edge, inside in ((0, 1), (LANES - 1, LANES - 2)):
-        packed = jnp.zeros((cells_x, LANES), F32)
-        for comp in range(3):
-            packed = jnp.where(at == comp, field[comp][:, edge : edge + 1], packed)
-            packed = jnp.where(at == 8 + comp, field[comp][:, inside : inside + 1], packed)
-        sides.append(packed)
-    turned = jnp.concatenate(sides, axis=0).T
-
-    def column_product(kind, first):
+    two = jnp.concatenate(field[:2], axis=0).T
+    third = jnp.concatenate([field[2], field[2]], axis=0).T
+
+    def column_rows(first, last):
+        low = lane_row < cells_x
+        one, other = two[first : first + 1], two[last : last + 1]
+        return [
+            jnp.where(low, one, pltpu.roll(other, cells_x, 1)),
+            jnp.where(low, pltpu.roll(one, cells_x, 1), other),
+            jnp.where(low, third[first : first + 1], third[last : last + 1]),
+        ]
+
+    edge = column_rows(0, LANES - 1)
+    inside = column_rows(1, LANES - 2)
+
+    def column_product(kind, rows):
         return sum(
-            columns_ref[8 * (kind + i) : 8 * (kind + i) + 8, :] * turned[first + i : first + i + 1]
-            for i in range(3)
+            columns_ref[8 * (kind + i) : 8 * (kind + i) + 8, :] * rows[i] for i in range(3)
         )
 
     def eight(rows):
@@ -371,18 +375,18 @@
         lane == LANES - 1, from_after, pltpu.roll(from_after, cells_x - 1, 1)
     )
     row = lane & (cells_x - 1)
-    upward = pltpu.roll(column_product(UP_X, 0), 1, 1)
-    downward = pltpu.roll(column_product(LOW_X, 0), LANES - 1, 1)
+    upward = pltpu.roll(column_product(UP_X, edge), 1, 1)
+    downward = pltpu.roll(column_product(LOW_X, edge), LANES - 1, 1)
     total = (
-        column_product(WITHIN, 0)
+        column_product(WITHIN, edge)
         + jnp.where(row == 0, from_before, upward)
         + jnp.where(row == cells_x - 1, from_after, downward)
-        + column_product(INWARD, 8)
+        + column_product(INWARD, inside)
     )
     inverse = columns_ref[8 * INVERSE : 8 * INVERSE + 8, :]
-    along_y, part = column_product(OUTWARD, 0), total * inverse
+    along_y, part = column_product(OUTWARD, edge), total * inverse
     stacked = jnp.concatenate(
-        [turned[:3], along_y[:3], part[:3], inverse[:3], jnp.zeros((4, LANES), F32)], axis=0
+        [*edge, along_y[:3], part[:3], inverse[:3], jnp.zeros((4, LANES), F32)], axis=0
     )
 
     def message(columns, end):

time: 34.8 us -> 34.7 us (level)
  transfers between devices with their start and end apart: 4 -> 4, of which waited for: 2 -> 2; matrix products, arithmetic and copies ran while one was open for 0% -> 0% of each run, Pallas kernels for 14% -> 13%
where the time goes in v5:
time: 34.7 us; the launch traced here: 34.4 us
  starting transfers between devices  12.7 us (37%)
  blocking collectives  9.69 us (28%)
  Pallas kernels  8.01 us (23%)
  waiting for transfers between devices  2.46 us (7%)
  between operations  1.53 us (4%)
    all_to_all x1, blocking collectives, per_device(): lax.all_to_all(partial, ('gx', 'gy'), split_axis=0, concat_axis=0, tiled=...  9.69 us
    all_to_all x1, starting transfers between devices, per_device(): rows = lax.all_to_all(rows, 'gx', split_axis=0, concat_axis=0, tiled=True)  5.19 us
    ppermute x2, starting transfers between devices, swapped(): return lax.ppermute(columns, 'gy', pairs)  5.12 us
    ppermute x1, starting transfers between devices, per_device(): strip = lax.ppermute(strip, 'gx', [(i, i + 1) for i in range(width_gx - 1)])  2.4 us
    all_to_all x1, waiting for transfers between devices, per_device(): rows = lax.all_to_all(rows, 'gx', split_axis=0, concat_axis=0, tiled=True)  2.31 us
    pallas_call x1, Pallas kernels, per_device(): pl.pallas_call(pack_kernel, in_specs=[SMEM] + [HBM] * 6, out_specs=[HBM,...  1.82 us
    pallas_call x1, Pallas kernels, per_device(): pl.pallas_call(field_kernel, in_specs=[VMEM] * 4, out_specs=[VMEM] * 4, o...  1.65 us
    pallas_call x1, Pallas kernels, per_device(): pl.pallas_call(functools.partial(box_kernel, tile_points=points // tiles)...  1.44 us
  transfers between devices with their start and end apart: 4, of which 2 were waited for; matrix products, arithmetic and copies ran while one was open for 0% of the time, Pallas kernels for 13%

profile of v5, /device:TPU:0, one launch (start us, length us, event | category | flops | bytes accessed | tf_op | source)
XLA Modules:
  0.0 34.4 jit_solution(7063837298908841804)
XLA Ops:
  0.6 0.0 copy-start.2
  0.6 0.0 copy-start
  0.7 0.0 copy-start.1
  1.4 1.8 %pack_rows_and_edges.1 = (f32[8,48,128]{2,1,0:T(8,128)}, f32[32,128]{1,0:T(8,128)S(1)}) custom-call(s32[1]{0:T(128)S(6)} %copy.12.count_ref, f32[3,1024]{1,0:T(4,128)} %values_in.1, s32[8,128]{1,0:T(8,128)} %bitcast.6, s32[8,128]{1,0:T(8,128)} %bitcast.7, f32[9,64,128]{2,1,0:T(8,128)} %diag_ref.5, f32[4,9,64,128]{3,2,1,0:T(8,128)} %edge_ref.5, ...), custom_call_target="tpu_custom_call" | custom-call | tf_op jit(solution)/shard_map/pack_rows_and_edges/pallas_call | solution.py:753
  3.3 5.2 %all-to-all-start = ((f32[8,48,128]{2,1,0:T(8,128)}), f32[8,48,128]{2,1,0:T(8,128)S(1)}, u32[]{:S(2)}, u32[]{:S(2)}) async-start(f32[8,48,128]{2,1,0:T(8,128)} %get-tuple-element.18), calls=%async_computation | async-start | bytes 393216 | tf_op jit(solution)/shard_map/all_to_all | solution.py:783
  8.4 0.0 copy-done.2
  8.5 0.0 copy-start.3
  8.5 0.0 copy-start.4
  8.5 0.0 copy-start.5
  8.5 1.1 %edge_columns.1 = (f32[3,64,128]{2,1,0:T(8,128)S(1)}, f32[128,128]{1,0:T(8,128)S(1)}, f32[40,128]{1,0:T(8,128)S(1)}) custom-call(f32[9,64,128]{2,1,0:T(8,128)S(1)} %copy-done.1, f32[4,9,64,128]{3,2,1,0:T(8,128)S(1)} %copy-done, s32[4,64,128]{2,1,0:T(8,128)S(1)} %copy-done.2), custom_call_target="tpu_custom_call" | custom-call | flops 100000000 | bytes 4000000 | tf_op jit(solution)/shard_map/edge_columns/pallas_call | solution.py:786
  9.6 2.4 %collective-permute-start.2 = (f32[40,128]{1,0:T(8,128)S(1)}, f32[40,128]{1,0:T(8,128)S(1)}, u32[]{:S(2)}, u32[]{:S(2)}) collective-permute-start(f32[40,128]{1,0:T(8,128)S(1)} %get-tuple-element.26), channel_id=1, source_target_pairs={{0,4},{4,8},{8,12},{12,16},{16,20},{20,24},{24,28},{1,5},{5,9},{9,... | collective-permute-start | bytes 61448 | tf_op jit(solution)/shard_map/ppermute | solution.py:797
  12.0 0.3 %own_load.1.own_ref = f32[208,256]{1,0:T(8,128)S(1)} custom-call(f32[32,128]{1,0:T(8,128)S(1)} %get-tuple-element.19.rows_ref), custom_call_target="tpu_custom_call" | custom-call | flops 100000000 | bytes 1000000 | tf_op jit(solution)/shard_map/own_load/pallas_call | solution.py:801
  12.4 2.3 %all-to-all-done.rows_ref = f32[8,48,128]{2,1,0:T(8,128)S(1)} async-done(((f32[8,48,128]{2,1,0:T(8,128)}), f32[8,48,128]{2,1,0:T(8,128)S(1)}, u32[]{:S(2)}, u32[]{:S(2)}) %all-to-all-start) | async-done | bytes 196640 | tf_op jit(solution)/shard_map/all_to_all | solution.py:783
  14.7 1.7 %load_and_first_product.1 = (f32[3,64,128]{2,1,0:T(8,128)S(1)}, f32[24,128]{1,0:T(8,128)S(1)}, f32[16,128]{1,0:T(8,128)S(1)}, f32[16,128]{1,0:T(8,128)S(1)}) custom-call(f32[8,48,128]{2,1,0:T(8,128)S(1)} %all-to-all-done.rows_ref, f32[208,256]{1,0:T(8,128)S(1)} %own_load.1.own_ref, f32[3,64,128]{2,1,0:T(8,128)S(1)} %get-tuple-element.20.inverse_ref, ...), custom_call_target="tpu_custom_call" | custom-call | tf_op jit(solution)/shard_map/load_and_first_product/pallas_call | solution.py:812
  16.3 0.7 %collective-permute-start = (f32[16,128]{1,0:T(8,128)S(1)}, f32[16,128]{1,0:T(8,128)S(1)}, u32[]{:S(2)}, u32[]{:S(2)}) collective-permute-start(f32[16,128]{1,0:T(8,128)S(1)} %get-tuple-element.22.inner_ref), channel_id=1, source_target_pairs={{1,2},{2,1},{5,6},{6,5},{9,10},{10,9},{13,14},{14,13},{17,18},{18,... | collective-permute-start | bytes 24584 | tf_op jit(solution)/shard_map/ppermute | solution.py:826
  17.0 4.5 %collective-permute-start.1 = (f32[16,128]{1,0:T(8,128)S(1)}, f32[16,128]{1,0:T(8,128)S(1)}, u32[]{:S(2)}, u32[]{:S(2)}) collective-permute-start(f32[16,128]{1,0:T(8,128)S(1)} %get-tuple-element.23.outer_ref), channel_id=1, source_target_pairs={{0,1},{2,3},{1,0},{3,2},{4,5},{6,7},{5,4},{7,6},{8,9},{10,11},{9,8... | collective-permute-start | bytes 24584 | tf_op jit(solution)/shard_map/ppermute | solution.py:826
  21.5 0.0 collective-permute-done.2.strip_ref
  21.5 0.0 copy-done.3
  21.5 1.4 %box_parts.1 = (f32[3,64,128]{2,1,0:T(8,128)S(1)}, f32[128,128]{1,0:T(8,128)S(1)}, bf16[128,2048]{1,0:T(8,128)(2,1)S(1)}, f32[8,128]{1,0:T(8,128)S(1)}, bf16[128,128]{1,0:T(8,128)(2,1)S(1)}) custom-call(s32[1,16]{1,0:T(1,128)S(1)} %bitcast.5, f32[3,64,128]{2,1,0:T(8,128)S(1)} %get-tuple-element.24.field_ref, s32[16,128]{1,0:T(8,128)S(1)} %bitcast.4, ...), custom_call_target="tpu_custom_call" | custom-call | flops 1000000000 | bytes 4000000 | tf_op jit(solution)/shard_map/box_parts/pallas_call | solution.py:830
  22.9 0.0 collective-permute-done.from_inner_ref
  22.9 0.1 collective-permute-done.1.from_outer_ref
  23.1 0.6 %sums_and_halo_parts.1 = (f32[3,64,128]{2,1,0:T(8,128)S(1)}, f32[32,4,128]{2,1,0:T(4,128)S(1)}) custom-call(f32[16,128]{1,0:T(8,128)S(1)} %collective-permute-done.from_inner_ref, f32[16,128]{1,0:T(8,128)S(1)} %collective-permute-done.1.from_outer_ref, f32[16,128]{1,0:T(8,128)S(1)} %get-tuple-element.22.inner_ref, ...), custom_call_target="tpu_custom_call" | custom-call | tf_op jit(solution)/shard_map/sums_and_halo_parts/pallas_call | solution.py:855
  23.7 9.7 %all_to_all.10.got_ref = f32[32,4,128]{2,1,0:T(4,128)S(1)} all-to-all(f32[32,4,128]{2,1,0:T(4,128)S(1)} %get-tuple-element.32), channel_id=1, replica_groups=mesh['gx'=8,'gy'=4] {'gx','gy'}, dimensions={0} | all-to-all | bytes 131072 | tf_op jit(solution)/shard_map/all_to_all | solution.py:866
  33.4 1.0 %steps_and_outputs.1 = (f32[3,64,128]{2,1,0:T(8,128)}, f32[1,192]{1,0:T(1,128)}) custom-call(f32[32,4,128]{2,1,0:T(4,128)S(1)} %all_to_all.10.got_ref, f32[3,64,128]{2,1,0:T(8,128)S(1)} %get-tuple-element.24.field_ref, f32[3,64,128]{2,1,0:T(8,128)S(1)} %get-tuple-element.33.quotient_ref), custom_call_target="tpu_custom_call" | custom-call | tf_op jit(solution)/shard_map/steps_and_outputs/pallas_call | solution.py:867
  (4 shorter events, 0.0 us)
Async XLA Ops:
  0.6 7.8 %copy-start.2 = (s32[4,64,128]{2,1,0:T(8,128)S(1)}, s32[4,64,128]{2,1,0:T(8,128)}, u32[]{:S(2)}) copy-start(s32[4,64,128]{2,1,0:T(8,128)} %mask_ref.5) | copy-start | bytes 393220
  0.6 7.8 %copy-start = (f32[4,9,64,128]{3,2,1,0:T(8,128)S(1)}, f32[4,9,64,128]{3,2,1,0:T(8,128)}, u32[]{:S(2)}) copy-start(f32[4,9,64,128]{3,2,1,0:T(8,128)} %edge_ref.5) | copy-start | bytes 3538948
  0.7 7.8 %copy-start.1 = (f32[9,64,128]{2,1,0:T(8,128)S(1)}, f32[9,64,128]{2,1,0:T(8,128)}, u32[]{:S(2)}) copy-start(f32[9,64,128]{2,1,0:T(8,128)} %diag_ref.5) | copy-start | bytes 884740
  3.3 11.4 %all-to-all-start = ((f32[8,48,128]{2,1,0:T(8,128)}), f32[8,48,128]{2,1,0:T(8,128)S(1)}, u32[]{:S(2)}, u32[]{:S(2)}) async-start(f32[8,48,128]{2,1,0:T(8,128)} %get-tuple-element.18), calls=%async_computation | async-start | bytes 393216 | tf_op jit(solution)/shard_map/all_to_all | solution.py:783
  8.5 13.0 %copy-start.3 = (f32[3,2048]{1,0:T(4,128)S(1)}, f32[3,2048]{1,0:T(4,128)}, u32[]{:S(2)}) copy-start(f32[3,2048]{1,0:T(4,128)} %param_ref.1) | copy-start | bytes 73732
  8.5 13.0 %copy-start.4 = (s32[2048]{0:T(1024)S(1)}, s32[2048]{0:T(1024)}, u32[]{:S(2)}) copy-start(s32[2048]{0:T(1024)} %param.17) | copy-start | bytes 24580
  8.5 13.0 %copy-start.5 = (s32[16]{0:T(128)S(1)}, s32[16]{0:T(128)}, u32[]{:S(2)}) copy-start(s32[16]{0:T(128)} %param.19) | copy-start | bytes 196
  9.6 11.9 %collective-permute-start.2 = (f32[40,128]{1,0:T(8,128)S(1)}, f32[40,128]{1,0:T(8,128)S(1)}, u32[]{:S(2)}, u32[]{:S(2)}) collective-permute-start(f32[40,128]{1,0:T(8,128)S(1)} %get-tuple-element.26), channel_id=1, source_target_pairs={{0,4},{4,8},{8,12},{12,16},{16,20},{20,24},{24,28},{1,5},{5,9},{9,... | collective-permute-start | bytes 61448 | tf_op jit(solution)/shard_map/ppermute | solution.py:797
  16.3 6.6 %collective-permute-start = (f32[16,128]{1,0:T(8,128)S(1)}, f32[16,128]{1,0:T(8,128)S(1)}, u32[]{:S(2)}, u32[]{:S(2)}) collective-permute-start(f32[16,128]{1,0:T(8,128)S(1)} %get-tuple-element.22.inner_ref), channel_id=1, source_target_pairs={{1,2},{2,1},{5,6},{6,5},{9,10},{10,9},{13,14},{14,13},{17,18},{18,... | collective-permute-start | bytes 24584 | tf_op jit(solution)/shard_map/ppermute | solution.py:826
  17.0 6.1 %collective-permute-start.1 = (f32[16,128]{1,0:T(8,128)S(1)}, f32[16,128]{1,0:T(8,128)S(1)}, u32[]{:S(2)}, u32[]{:S(2)}) collective-permute-start(f32[16,128]{1,0:T(8,128)S(1)} %get-tuple-element.23.outer_ref), channel_id=1, source_target_pairs={{0,1},{2,3},{1,0},{3,2},{4,5},{6,7},{5,4},{7,6},{8,9},{10,11},{9,8... | collective-permute-start | bytes 24584 | tf_op jit(solution)/shard_map/ppermute | solution.py:826

commit v6 on v5

--- a/solution.py
+++ b/solution.py
@@ -587,7 +587,7 @@
 
 def sums_kernel(
     from_inner_ref, from_outer_ref, inner_ref, outer_ref, field_ref, part_ref, halo_ref,
-    diag_ref, edge_ref, mask_ref, box_ref, adjoint_ref, before_ref, matrix_ref,
+    diag_ref, edge_ref, mask_ref, box_ref, adjoint_ref, before_ref, matrix_ref, columns_ref,
     quotient_ref, out_ref,
 ):
     cells_x = field_ref.shape[1]
@@ -607,40 +607,33 @@
             [row(arrived, 2, c) + row(arrived, 3, c) * row(own, 1, c) for c in range(3)]
         )
 
-    def turned(columns, share, edge):
-        kept = [
-            jnp.where(lane_row < cells_x, share[c], columns[3 + c : 4 + c]) for c in range(3)
-        ]
-        rest = jnp.zeros((LANES - 9, LANES), F32)
-        return jnp.concatenate([columns[:3], *kept, *edge, rest], axis=0).T
-
-    low = turned(from_low, shares[0], edges[0])
-    high = turned(from_high, shares[1], edges[1])
+    none = jnp.zeros((1, LANES), F32)
+    rest = jnp.zeros((LANES - 6, LANES), F32)
+    turned = jnp.concatenate([*shares[0], *shares[1], rest], axis=0).T
     lane = iota((cells_x, LANES), 1)
 
-    def column(source, slot, comp):
-        return source[:cells_x, 3 * slot + comp : 3 * slot + comp + 1]
+    def both(low, high):
+        return jnp.where(lane_row < cells_x, low, pltpu.roll(high, cells_x, 1))
 
     field = [field_ref[c] for c in range(3)]
     scale = [diag_ref[4 * c] for c in range(3)]
-    quotient, low_edge, high_edge = [], [], []
+    quotient = []
     for c in range(3):
         entering = jnp.where(
             lane == 0,
-            column(low, 1, c),
-            jnp.where(lane == LANES - 1, column(high, 1, c), 0.0),
+            turned[:cells_x, c : c + 1],
+            jnp.where(lane == LANES - 1, turned[:cells_x, 3 + c : 4 + c], 0.0),
         )
         quotient.append(part_ref[c] + entering)
-        low_edge.append(column(low, 2, c))
-        high_edge.append(column(high, 2, c))
-    for c in range(3):
         quotient_ref[c] = quotient[c]
     before, before_quotient = [], []
     for c in range(3):
         entering = jnp.where(
             lane_row == 0,
-            low[cells_x : cells_x + 1, 3 + c : 4 + c],
-            jnp.where(lane_row == LANES - 1, high[cells_x : cells_x + 1, 3 + c : 4 + c], 0.0),
+            from_low[3 + c : 4 + c, cells_x : cells_x + 1],
+            jnp.where(
+                lane_row == LANES - 1, from_high[3 + c : 4 + c, cells_x : cells_x + 1], 0.0
+            ),
         )
         before.append(halo_ref[c : c + 1, :])
         before_quotient.append(
@@ -661,7 +654,6 @@
         (pltpu.roll, LANES - 1, 1, lane == LANES - 1),
     )
     extra = [0.0, 0.0]
-    sides = [0.0, 0.0]
     for direction, (roll, step, dim, edge) in enumerate(moves):
         moving = masked_product(edge_ref, mask_ref, direction, quotient)
         for c in range(3):
@@ -671,28 +663,28 @@
             if direction == 1:
                 extra[0] += moving[c][:1] * before[c]
                 extra[1] += moving[c][:1] * before_quotient[c]
-            elif direction == 2:
-                sides[0] += moving[c][:, LANES - 1 :] * column(high, 0, c)
-                sides[1] += moving[c][:, LANES - 1 :] * high_edge[c]
-            elif direction == 3:
-                sides[0] += moving[c][:, :1] * column(low, 0, c)
-                sides[1] += moving[c][:, :1] * low_edge[c]
+    at_edge = [
+        both(first[6 + c : 7 + c] + shares[0][c], last[6 + c : 7 + c] + shares[1][c])
+        for c in range(3)
+    ]
+    leaving = sum(
+        columns_ref[8 * (OUTWARD + i) : 8 * (OUTWARD + i) + 8, :] * at_edge[i]
+        for i in range(3)
+    )
+    for c in range(3):
+        out = leaving[c : c + 1]
+        extra[0] += out * both(from_low[c : c + 1], from_high[c : c + 1])
+        extra[1] += out * both(edges[0][c], edges[1][c])
     incoming = product(lambda k: halo_ref[9 + k : 10 + k, :], before_quotient)
     extra[0] += sum(incoming[c] * field[c][:1] for c in range(3))
     extra[1] += sum(incoming[c] * quotient[c][:1] for c in range(3))
-    fourth_sum = fourth_sum + jnp.where(lane == 0, sides[0], 0.0)
-    fifth_sum = fifth_sum + jnp.where(lane == 0, sides[1], 0.0)
     extra = [0.0, 0.0, 0.0, extra[0], extra[1]]
     sums = jnp.zeros((1, LANES), F32)
     for k, value in enumerate((first_sum, second_sum, third_sum, fourth_sum, fifth_sum)):
         line = jnp.sum(value, axis=0, keepdims=True) + extra[k]
         sums = jnp.where(lane_row == k, jnp.sum(line, axis=1, keepdims=True), sums)
 
-    added = [
-        jnp.where(lane_row < cells_x, shares[0][c], pltpu.roll(shares[1][c], cells_x, 1))
-        for c in range(3)
-    ]
-    none = jnp.zeros((1, LANES), F32)
+    added = [both(shares[0][c], shares[1][c]) for c in range(3)]
     added = jnp.concatenate(
         [none, added[0], none, none, none, added[1], added[2], none], axis=0
     )
@@ -854,14 +846,14 @@
 
     quotient, partial = pl.pallas_call(
         sums_kernel,
-        in_specs=[VMEM] * 14,
+        in_specs=[VMEM] * 15,
         out_specs=[VMEM] * 2,
         out_shape=[whole(nodes), whole((devices, 4, LANES))],
         compiler_params=PARAMS,
         name="sums_and_halo_parts",
     )(
         from_inner, from_outer, inner, outer, field, part, halo, diag_blocks, edge_blocks, edge_mask,
-        box_part, adjoint, before, matrix,
+        box_part, adjoint, before, matrix, columns,
     )
     got = lax.all_to_all(partial, ("gx", "gy"), split_axis=0, concat_axis=0, tiled=True)
     return pl.pallas_call(

time: 34.7 us -> 34.7 us (level)
  no operation moved by 1% of the time
where the time goes in v6:
time: 34.7 us; the launch traced here: 34.4 us
  starting transfers between devices  12.7 us (37%)
  blocking collectives  9.69 us (28%)
  Pallas kernels  8.02 us (23%)
  waiting for transfers between devices  2.46 us (7%)
  between operations  1.53 us (4%)
    all_to_all x1, blocking collectives, per_device(): lax.all_to_all(partial, ('gx', 'gy'), split_axis=0, concat_axis=0, tiled=...  9.69 us
    all_to_all x1, starting transfers between devices, per_device(): rows = lax.all_to_all(rows, 'gx', split_axis=0, concat_axis=0, tiled=True)  5.19 us
    ppermute x2, starting transfers between devices, swapped(): return lax.ppermute(columns, 'gy', pairs)  5.12 us
    ppermute x1, starting transfers between devices, per_device(): strip = lax.ppermute(strip, 'gx', [(i, i + 1) for i in range(width_gx - 1)])  2.4 us
    all_to_all x1, waiting for transfers between devices, per_device(): rows = lax.all_to_all(rows, 'gx', split_axis=0, concat_axis=0, tiled=True)  2.31 us
    pallas_call x1, Pallas kernels, per_device(): pl.pallas_call(pack_kernel, in_specs=[SMEM] + [HBM] * 6, out_specs=[HBM,...  1.82 us
    pallas_call x1, Pallas kernels, per_device(): pl.pallas_call(field_kernel, in_specs=[VMEM] * 4, out_specs=[VMEM] * 4, o...  1.65 us
    pallas_call x1, Pallas kernels, per_device(): pl.pallas_call(functools.partial(box_kernel, tile_points=points // tiles)...  1.44 us
  transfers between devices with their start and end apart: 4, of which 2 were waited for; matrix products, arithmetic and copies ran while one was open for 0% of the time, Pallas kernels for 13%

profile of v6, /device:TPU:0, one launch (start us, length us, event | category | flops | bytes accessed | tf_op | source)
XLA Modules:
  0.0 34.4 jit_solution(10112519835187055468)
XLA Ops:
  0.6 0.0 copy-start.2
  0.6 0.0 copy-start
  0.7 0.0 copy-start.1
  1.4 1.8 %pack_rows_and_edges.1 = (f32[8,48,128]{2,1,0:T(8,128)}, f32[32,128]{1,0:T(8,128)S(1)}) custom-call(s32[1]{0:T(128)S(6)} %copy.12.count_ref, f32[3,1024]{1,0:T(4,128)} %values_in.1, s32[8,128]{1,0:T(8,128)} %bitcast.6, s32[8,128]{1,0:T(8,128)} %bitcast.7, f32[9,64,128]{2,1,0:T(8,128)} %diag_ref.5, f32[4,9,64,128]{3,2,1,0:T(8,128)} %edge_ref.5, ...), custom_call_target="tpu_custom_call" | custom-call | tf_op jit(solution)/shard_map/pack_rows_and_edges/pallas_call | solution.py:745
  3.3 5.2 %all-to-all-start = ((f32[8,48,128]{2,1,0:T(8,128)}), f32[8,48,128]{2,1,0:T(8,128)S(1)}, u32[]{:S(2)}, u32[]{:S(2)}) async-start(f32[8,48,128]{2,1,0:T(8,128)} %get-tuple-element.18), calls=%async_computation | async-start | bytes 393216 | tf_op jit(solution)/shard_map/all_to_all | solution.py:775
  8.4 0.0 copy-done.2
  8.5 0.0 copy-start.3
  8.5 0.0 copy-start.4
  8.5 0.0 copy-start.5
  8.5 1.1 %edge_columns.1 = (f32[3,64,128]{2,1,0:T(8,128)S(1)}, f32[128,128]{1,0:T(8,128)S(1)}, f32[40,128]{1,0:T(8,128)S(1)}) custom-call(f32[9,64,128]{2,1,0:T(8,128)S(1)} %copy-done.1, f32[4,9,64,128]{3,2,1,0:T(8,128)S(1)} %copy-done, s32[4,64,128]{2,1,0:T(8,128)S(1)} %copy-done.2), custom_call_target="tpu_custom_call" | custom-call | flops 100000000 | bytes 4000000 | tf_op jit(solution)/shard_map/edge_columns/pallas_call | solution.py:778
  9.6 2.4 %collective-permute-start.2 = (f32[40,128]{1,0:T(8,128)S(1)}, f32[40,128]{1,0:T(8,128)S(1)}, u32[]{:S(2)}, u32[]{:S(2)}) collective-permute-start(f32[40,128]{1,0:T(8,128)S(1)} %get-tuple-element.26), channel_id=1, source_target_pairs={{0,4},{4,8},{8,12},{12,16},{16,20},{20,24},{24,28},{1,5},{5,9},{9,... | collective-permute-start | bytes 61448 | tf_op jit(solution)/shard_map/ppermute | solution.py:789
  12.0 0.3 %own_load.1.own_ref = f32[208,256]{1,0:T(8,128)S(1)} custom-call(f32[32,128]{1,0:T(8,128)S(1)} %get-tuple-element.19.rows_ref), custom_call_target="tpu_custom_call" | custom-call | flops 100000000 | bytes 1000000 | tf_op jit(solution)/shard_map/own_load/pallas_call | solution.py:793
  12.4 2.3 %all-to-all-done.rows_ref = f32[8,48,128]{2,1,0:T(8,128)S(1)} async-done(((f32[8,48,128]{2,1,0:T(8,128)}), f32[8,48,128]{2,1,0:T(8,128)S(1)}, u32[]{:S(2)}, u32[]{:S(2)}) %all-to-all-start) | async-done | bytes 196640 | tf_op jit(solution)/shard_map/all_to_all | solution.py:775
  14.7 1.7 %load_and_first_product.1 = (f32[3,64,128]{2,1,0:T(8,128)S(1)}, f32[24,128]{1,0:T(8,128)S(1)}, f32[16,128]{1,0:T(8,128)S(1)}, f32[16,128]{1,0:T(8,128)S(1)}) custom-call(f32[8,48,128]{2,1,0:T(8,128)S(1)} %all-to-all-done.rows_ref, f32[208,256]{1,0:T(8,128)S(1)} %own_load.1.own_ref, f32[3,64,128]{2,1,0:T(8,128)S(1)} %get-tuple-element.20.inverse_ref, ...), custom_call_target="tpu_custom_call" | custom-call | tf_op jit(solution)/shard_map/load_and_first_product/pallas_call | solution.py:804
  16.3 0.7 %collective-permute-start = (f32[16,128]{1,0:T(8,128)S(1)}, f32[16,128]{1,0:T(8,128)S(1)}, u32[]{:S(2)}, u32[]{:S(2)}) collective-permute-start(f32[16,128]{1,0:T(8,128)S(1)} %get-tuple-element.22.inner_ref), channel_id=1, source_target_pairs={{1,2},{2,1},{5,6},{6,5},{9,10},{10,9},{13,14},{14,13},{17,18},{18,... | collective-permute-start | bytes 24584 | tf_op jit(solution)/shard_map/ppermute | solution.py:818
  17.0 4.5 %collective-permute-start.1 = (f32[16,128]{1,0:T(8,128)S(1)}, f32[16,128]{1,0:T(8,128)S(1)}, u32[]{:S(2)}, u32[]{:S(2)}) collective-permute-start(f32[16,128]{1,0:T(8,128)S(1)} %get-tuple-element.23.outer_ref), channel_id=1, source_target_pairs={{0,1},{2,3},{1,0},{3,2},{4,5},{6,7},{5,4},{7,6},{8,9},{10,11},{9,8... | collective-permute-start | bytes 24584 | tf_op jit(solution)/shard_map/ppermute | solution.py:818
  21.5 0.0 collective-permute-done.2.strip_ref
  21.5 0.0 copy-done.3
  21.5 1.4 %box_parts.1 = (f32[3,64,128]{2,1,0:T(8,128)S(1)}, f32[128,128]{1,0:T(8,128)S(1)}, bf16[128,2048]{1,0:T(8,128)(2,1)S(1)}, f32[8,128]{1,0:T(8,128)S(1)}, bf16[128,128]{1,0:T(8,128)(2,1)S(1)}) custom-call(s32[1,16]{1,0:T(1,128)S(1)} %bitcast.5, f32[3,64,128]{2,1,0:T(8,128)S(1)} %get-tuple-element.24.field_ref, s32[16,128]{1,0:T(8,128)S(1)} %bitcast.4, ...), custom_call_target="tpu_custom_call" | custom-call | flops 1000000000 | bytes 4000000 | tf_op jit(solution)/shard_map/box_parts/pallas_call | solution.py:822
  22.9 0.0 collective-permute-done.from_inner_ref
  22.9 0.1 collective-permute-done.1.from_outer_ref
  23.1 0.6 %sums_and_halo_parts.1 = (f32[3,64,128]{2,1,0:T(8,128)S(1)}, f32[32,4,128]{2,1,0:T(4,128)S(1)}) custom-call(f32[16,128]{1,0:T(8,128)S(1)} %collective-permute-done.from_inner_ref, f32[16,128]{1,0:T(8,128)S(1)} %collective-permute-done.1.from_outer_ref, f32[16,128]{1,0:T(8,128)S(1)} %get-tuple-element.22.inner_ref, ...), custom_call_target="tpu_custom_call" | custom-call | tf_op jit(solution)/shard_map/sums_and_halo_parts/pallas_call | solution.py:847
  23.7 9.7 %all_to_all.10.got_ref = f32[32,4,128]{2,1,0:T(4,128)S(1)} all-to-all(f32[32,4,128]{2,1,0:T(4,128)S(1)} %get-tuple-element.32), channel_id=1, replica_groups=mesh['gx'=8,'gy'=4] {'gx','gy'}, dimensions={0} | all-to-all | bytes 131072 | tf_op jit(solution)/shard_map/all_to_all | solution.py:858
  33.4 1.0 %steps_and_outputs.1 = (f32[3,64,128]{2,1,0:T(8,128)}, f32[1,192]{1,0:T(1,128)}) custom-call(f32[32,4,128]{2,1,0:T(4,128)S(1)} %all_to_all.10.got_ref, f32[3,64,128]{2,1,0:T(8,128)S(1)} %get-tuple-element.24.field_ref, f32[3,64,128]{2,1,0:T(8,128)S(1)} %get-tuple-element.33.quotient_ref), custom_call_target="tpu_custom_call" | custom-call | tf_op jit(solution)/shard_map/steps_and_outputs/pallas_call | solution.py:859
  (4 shorter events, 0.0 us)
Async XLA Ops:
  0.6 7.8 %copy-start.2 = (s32[4,64,128]{2,1,0:T(8,128)S(1)}, s32[4,64,128]{2,1,0:T(8,128)}, u32[]{:S(2)}) copy-start(s32[4,64,128]{2,1,0:T(8,128)} %mask_ref.5) | copy-start | bytes 393220
  0.6 7.8 %copy-start = (f32[4,9,64,128]{3,2,1,0:T(8,128)S(1)}, f32[4,9,64,128]{3,2,1,0:T(8,128)}, u32[]{:S(2)}) copy-start(f32[4,9,64,128]{3,2,1,0:T(8,128)} %edge_ref.5) | copy-start | bytes 3538948
  0.7 7.8 %copy-start.1 = (f32[9,64,128]{2,1,0:T(8,128)S(1)}, f32[9,64,128]{2,1,0:T(8,128)}, u32[]{:S(2)}) copy-start(f32[9,64,128]{2,1,0:T(8,128)} %diag_ref.5) | copy-start | bytes 884740
  3.3 11.4 %all-to-all-start = ((f32[8,48,128]{2,1,0:T(8,128)}), f32[8,48,128]{2,1,0:T(8,128)S(1)}, u32[]{:S(2)}, u32[]{:S(2)}) async-start(f32[8,48,128]{2,1,0:T(8,128)} %get-tuple-element.18), calls=%async_computation | async-start | bytes 393216 | tf_op jit(solution)/shard_map/all_to_all | solution.py:775
  8.5 13.0 %copy-start.3 = (f32[3,2048]{1,0:T(4,128)S(1)}, f32[3,2048]{1,0:T(4,128)}, u32[]{:S(2)}) copy-start(f32[3,2048]{1,0:T(4,128)} %param_ref.1) | copy-start | bytes 73732
  8.5 13.0 %copy-start.4 = (s32[2048]{0:T(1024)S(1)}, s32[2048]{0:T(1024)}, u32[]{:S(2)}) copy-start(s32[2048]{0:T(1024)} %param.17) | copy-start | bytes 24580
  8.5 13.0 %copy-start.5 = (s32[16]{0:T(128)S(1)}, s32[16]{0:T(128)}, u32[]{:S(2)}) copy-start(s32[16]{0:T(128)} %param.19) | copy-start | bytes 196
  9.6 11.9 %collective-permute-start.2 = (f32[40,128]{1,0:T(8,128)S(1)}, f32[40,128]{1,0:T(8,128)S(1)}, u32[]{:S(2)}, u32[]{:S(2)}) collective-permute-start(f32[40,128]{1,0:T(8,128)S(1)} %get-tuple-element.26), channel_id=1, source_target_pairs={{0,4},{4,8},{8,12},{12,16},{16,20},{20,24},{24,28},{1,5},{5,9},{9,... | collective-permute-start | bytes 61448 | tf_op jit(solution)/shard_map/ppermute | solution.py:789
  16.3 6.6 %collective-permute-start = (f32[16,128]{1,0:T(8,128)S(1)}, f32[16,128]{1,0:T(8,128)S(1)}, u32[]{:S(2)}, u32[]{:S(2)}) collective-permute-start(f32[16,128]{1,0:T(8,128)S(1)} %get-tuple-element.22.inner_ref), channel_id=1, source_target_pairs={{1,2},{2,1},{5,6},{6,5},{9,10},{10,9},{13,14},{14,13},{17,18},{18,... | collective-permute-start | bytes 24584 | tf_op jit(solution)/shard_map/ppermute | solution.py:818
  17.0 6.1 %collective-permute-start.1 = (f32[16,128]{1,0:T(8,128)S(1)}, f32[16,128]{1,0:T(8,128)S(1)}, u32[]{:S(2)}, u32[]{:S(2)}) collective-permute-start(f32[16,128]{1,0:T(8,128)S(1)} %get-tuple-element.23.outer_ref), channel_id=1, source_target_pairs={{0,1},{2,3},{1,0},{3,2},{4,5},{6,7},{5,4},{7,6},{8,9},{10,11},{9,8... | collective-permute-start | bytes 24584 | tf_op jit(solution)/shard_map/ppermute | solution.py:818
